TPU v7x, 128 devices: a whole 4x4x4 slice. The times are simulated.
128 devices in a mesh: grp: 4 (over x), dev: 32 (over z, y, core).
Axes of the slice: x: 4, y: 4, z: 4, core: 2. Of those that a mesh axis runs over, the one named last changes fastest.
Arguments:
- populations: float32 [19, 128, 8, 4096], P(None, 'grp', None, 'dev'), as said below
- fill: float32 [128, 8, 4096], P('grp', None, 'dev'), may hold values from 0 to 1, as said below
- flags: int32 [128, 8, 4096], P('grp', None, 'dev'), may hold values from 0 to 2, as said below
- specific_energy_grid: float32 [128, 8, 4096], P(('grp', 'dev')), may hold values from 0 to 2.5
Outputs:
- populations_out: float32 [19, 128, 8, 4096], P(None, 'grp', None, 'dev')
- fill_out: float32 [128, 8, 4096], P('grp', None, 'dev')
- enthalpy_out: float32 [128, 8, 4096], P(('grp', 'dev'))
Inputs may be any that keep to these rules, and one draw needn't show every extreme that they name: flags is 0 on gas, 1 on interface, 2 on liquid cells. fill is exactly 0 on gas cells, exactly 1 on liquid cells, and between 0.02 and 0.98 on interface cells. `populations`: every population is positive, within 0.5 and 1.5 times its lattice weight.
All inputs are finite; a program needn't handle non-finite values.
Results may differ from a plain program's by a relative error of at most 0.0003.
Values sent between devices are 32-bit elements; how exact they have to be, the bound alone decides.
A program may use at most 128 MiB of HBM per device.

v0:
```python
import functools

import jax
import jax.numpy as jnp
from jax import lax
from jax.experimental import pallas as pl
from jax.experimental.pallas import tpu as pltpu
from jax.sharding import PartitionSpec as P

MESH = pl.DeviceIdType.MESH
F32 = jnp.float32
VELOCITIES = (
    (0, 0, 0),
    (1, 0, 0),
    (-1, 0, 0),
    (0, 1, 0),
    (0, -1, 0),
    (0, 0, 1),
    (0, 0, -1),
    (1, 1, 0),
    (-1, -1, 0),
    (1, -1, 0),
    (-1, 1, 0),
    (1, 0, 1),
    (-1, 0, -1),
    (1, 0, -1),
    (-1, 0, 1),
    (0, 1, 1),
    (0, -1, -1),
    (0, 1, -1),
    (0, -1, 1),
)
WEIGHTS = (1.0 / 3.0,) + (1.0 / 18.0,) * 6 + (1.0 / 36.0,) * 12
RELAX_TIME = 0.8
GRAVITY = -0.002
STEP_TIME = 0.2

NG, ND, NP, NY, NL = 4, 32, 32, 8, 128
FLAT = (1, 2, 3, 4, 7, 8, 9, 10)
UP = (5, 15, 18, 11, 14)
DOWN = (6, 16, 17, 13, 12)
CROSS = UP + DOWN
EAST = (1, 7, 9, 11, 13)
WEST = (2, 8, 10, 12, 14)
Z_PAIRS = (5, 11, 13, 15, 17)


def opposite(q):
    return q + 1 if q % 2 == 1 else q - 1


def lane_iota():
    return lax.broadcasted_iota(jnp.int32, (NY, NL), 1)


def shift_rows(x, cy):
    return x if cy == 0 else pltpu.roll(x, cy % NY, 0)


def spread(x, lane):
    return jnp.broadcast_to(x[:, lane : lane + 1], (NY, NL))


def moments(d, s):
    out = []
    for axis in range(3):
        total = None
        for q, diff in d.items():
            c = VELOCITIES[q][axis]
            if c == 0:
                continue
            if total is None:
                total = diff if c > 0 else -diff
            else:
                total = total + diff if c > 0 else total - diff
        out.append(total)
    return out, sum(s.values())


def pack_columns(tops, bottoms, fill, p, acc, lane):
    spot = lane & 31
    here = spot == p
    east = lane == ((p + 1) & 31)
    west = lane == 32 + ((p + 31) & 31)
    out = []
    for side, (cols, edge) in enumerate(((tops, NL - 1), (bottoms, 0))):
        a, b = acc[2 * side], acc[2 * side + 1]
        v = spread(cols[0], edge)
        v = jnp.where(lane >= 32, spread(cols[1], edge), v)
        v = jnp.where(lane >= 64, spread(cols[2], edge), v)
        v = jnp.where(lane >= 96, spread(fill, edge), v)
        a = jnp.where(here, v, a)
        b = jnp.where(east, spread(cols[3], edge), b)
        b = jnp.where(west, spread(cols[4], edge), b)
        out += [a, b]
    return tuple(out)


def fluid_kernel(
    pops_in, fill_in, flags_in, energy_in,
    pops_out, fill_out, warm_out,
    f0, f1, fz0, fz1, fz2, roll_z, g_s, part, eqs, flags, vel, heat_pad, heat_d,
    xs, xr, zs, zr, zd, hx, hzs, hzr, msg,
    load_sem, send_sem, recv_sem, hot_sem, hsend_sem, hrecv_sem, aout_sem, out_sem,
):
    g, d = lax.axis_index("grp"), lax.axis_index("dev")
    up, down = lax.rem(d + 1, ND), lax.rem(d + ND - 1, ND)
    east, west = lax.rem(g + 1, NG), lax.rem(g + NG - 1, NG)
    lane = lane_iota()

    loads = [
        pltpu.make_async_copy(pops_in, f0.at[:, pl.ds(1, NP)], load_sem.at[0]),
        pltpu.make_async_copy(fill_in, fz0.at[1, pl.ds(1, NP), pl.ds(8, 8)], load_sem.at[1]),
        pltpu.make_async_copy(flags_in, flags, load_sem.at[2]),
    ]
    for c in loads:
        c.start()

    barrier = pltpu.get_barrier_semaphore()

    def greet(i, c):
        pl.semaphore_signal(barrier, inc=1, device_id=(g, lax.rem(d + i, ND)), device_id_type=MESH)
        return c

    lax.fori_loop(1, ND, greet, 0)
    for gg in (east, west):
        for dd in (d, up, down):
            pl.semaphore_signal(barrier, inc=1, device_id=(gg, dd), device_id_type=MESH)

    zero8 = jnp.zeros((NY, NL), F32)

    def clear(p, c):
        for ref in (fz0, fz1, fz2):
            for k in range(3):
                ref[k, p, 0:8] = zero8
                ref[k, p, 16:24] = zero8
        for k in range(2):
            heat_pad[k, p, 0:8] = zero8
            heat_pad[k, p, 16:24] = zero8
        return c

    lax.fori_loop(0, NP + 2, clear, 0)

    for c in loads:
        c.wait()

    def send(t, src, dst, n, to):
        return pltpu.make_async_remote_copy(
            src_ref=src, dst_ref=dst, send_sem=send_sem.at[t, n], recv_sem=recv_sem.at[t, n],
            device_id=to, device_id_type=MESH,
        )

    def x_sends(t):
        return [
            send(t, xs.at[t, 0], xr.at[t, 0], 0, (east, d)),
            send(t, xs.at[t, 1], xr.at[t, 1], 1, (west, d)),
        ]

    def z_sends(t):
        out = []
        for side, to in ((0, up), (1, down)):
            out.append(send(t, zs.at[t, side], zr.at[t, side], 2 + 3 * side, (g, to)))
            out.append(send(t, zs.at[t, side], zd.at[t, side, 0], 3 + 3 * side, (east, to)))
            out.append(send(t, zs.at[t, side], zd.at[t, side, 1], 4 + 3 * side, (west, to)))
        return out

    def fill_x(t, f, fz):
        for k, q in enumerate(EAST):
            xs[t, 0, k] = f[q, NP]
        xs[t, 0, 5] = fz[1, NP, 8:16]
        for k, q in enumerate(WEST):
            xs[t, 1, k] = f[q, 1]
        xs[t, 1, 5] = fz[1, 1, 8:16]

    def store_z(t, acc):
        for side in range(2):
            zs[t, side, 0:8] = acc[2 * side]
            zs[t, side, 8:16] = acc[2 * side + 1]

    fill_x(0, f0, fz0)

    def pack0(p, acc):
        return pack_columns(
            [f0[q, p + 1] for q in UP], [f0[q, p + 1] for q in DOWN], fz0[1, p + 1, 8:16], p, acc, lane
        )

    acc0 = (zero8,) * 4
    store_z(0, lax.fori_loop(0, NP, pack0, acc0, unroll=4))

    pl.semaphore_wait(barrier, 37)
    pending = z_sends(0) + x_sends(0)
    for c in pending:
        c.start()

    def hot(i, to):
        return pltpu.make_async_remote_copy(
            src_ref=energy_in.at[0, :, pl.ds(pl.multiple_of(to * NL, NL), NL)],
            dst_ref=heat_pad.at[0, d + 1, pl.ds(8, 8)],
            send_sem=hot_sem.at[0], recv_sem=hot_sem.at[1], device_id=(g, to), device_id_type=MESH,
        )

    def hot_start(i, c):
        hot(i, lax.rem(d + i, ND)).start()
        return c

    lax.fori_loop(1, ND, hot_start, 0)
    own = pltpu.make_async_copy(
        energy_in.at[0, :, pl.ds(pl.multiple_of(d * NL, NL), NL)],
        heat_pad.at[0, d + 1, pl.ds(8, 8)], load_sem.at[3],
    )
    own.start()

    def local_part(f, fz):
        def body(p):
            pops = [f[q, p + 1] for q in range(19)]
            kind = flags[p]
            gas = kind == 0
            fill = fz[1, p + 1, 8:16]
            diffs = {q: pops[q] - pops[q + 1] for q in range(1, 19, 2)}
            sums = {q: pops[q] + pops[q + 1] for q in range(1, 19, 2)}
            (mx, my, mz), total = moments(diffs, sums)
            dens = jnp.where(gas, 1.0, total + pops[0])
            inv = 1.0 / dens
            vx, vy, vz = mx * inv, my * inv, mz * inv
            base = 1.0 - 1.5 * (vx * vx + vy * vy + vz * vz)

            def paired(q):
                cx, cy, cz = VELOCITIES[q]
                along = None
                for c, v in ((cx, vx), (cy, vy), (cz, vz)):
                    if c:
                        along = (v if c > 0 else -v) if along is None else (along + v if c > 0 else along - v)
                return (2.0 * WEIGHTS[q]) * (base + 4.5 * along * along)

            for k, q in enumerate(Z_PAIRS):
                eqs[k, p] = paired(q)
            for k, q in enumerate(CROSS):
                roll_z[k, p + 1] = pltpu.roll(pops[q], 1 if q in UP else NL - 1, 1)
            ex = None
            got = {0: pops[0]}
            for q in FLAT:
                cx, cy, _ = VELOCITIES[q]
                incoming = shift_rows(f[q, p + 1 - cx], cy)
                beside = fz[1, p + 1 - cx, 8 - cy : 16 - cy]
                empty = beside == 0.0
                back = pops[opposite(q)]
                got[q] = jnp.where(empty, paired(q if q % 2 else q - 1) - back, incoming)
                term = jnp.where(empty, 0.0, (fill + beside) * (incoming - back))
                ex = term if ex is None else ex + term
                g_s[q, p] = got[q]
            diffs = {q: got[q] - got[q + 1] for q in FLAT if q % 2}
            sums = {q: got[q] + got[q + 1] for q in FLAT if q % 2}
            (mx, my, _), total = moments(diffs, sums)
            part[0, p] = total + got[0]
            part[1, p] = mx
            part[2, p] = my
            part[3, p] = fill * dens + 0.5 * ex

        return body

    def arrive_x(t, f, fz):
        not_first, not_last = g > 0, g < NG - 1
        for k, q in enumerate(EAST):
            f[q, 0] = xr[t, 0, k]
        for k, q in enumerate(WEST):
            f[q, NP + 1] = xr[t, 1, k]
        fz[1, 0, 8:16] = jnp.where(not_first, xr[t, 0, 5], 0.0)
        fz[1, NP + 1, 8:16] = jnp.where(not_last, xr[t, 1, 5], 0.0)
        for q in (11, 13):
            roll_z[CROSS.index(q), 0] = pltpu.roll(f[q, 0], 1 if q in UP else NL - 1, 1)
        for q in (12, 14):
            roll_z[CROSS.index(q), NP + 1] = pltpu.roll(f[q, NP + 1], 1 if q in UP else NL - 1, 1)

    def arrive_z(t, fz):
        for side in range(2):
            inside = d > 0 if side == 0 else d < ND - 1
            main0, main1 = zr[t, side, 0:8], zr[t, side, 8:16]
            b = jnp.where(lane == 0, zd[t, side, 0, 8:16], main1)
            b = jnp.where(lane == 63, zd[t, side, 1, 8:16], b)
            zr[t, side, 8:16] = b
            edge = 0 if side == 0 else NL - 1
            k = 0 if side == 0 else 2
            by = 1 if side == 0 else NL - 1

            def column(p, c):
                old = pltpu.roll(fz[1, p + 1, 8:16], by, 1)
                new = pltpu.roll(main0, lax.rem(NL + edge - 96 - p, NL), 1)
                fz[k, p + 1, 8:16] = jnp.where(lane == edge, jnp.where(inside, new, 0.0), old)
                return c

            lax.fori_loop(0, NP, column, 0, unroll=8)
            for at, src, spot, ok in ((0, 0, 127, g > 0), (NP + 1, 1, 96, g < NG - 1)):
                old = pltpu.roll(fz[1, at, 8:16], by, 1)
                new = spread(zd[t, side, src, 0:8], spot)
                ok = jnp.logical_and(ok, inside)
                fz[k, at, 8:16] = jnp.where(lane == edge, jnp.where(ok, new, 0.0), old)

    def cross_part(t, f, fz, p):
        kind = flags[p]
        gas = kind == 0
        fill = fz[1, p + 1, 8:16]
        got = {}
        ex = None
        for side, dirs in enumerate((UP, DOWN)):
            edge = 0 if side == 0 else NL - 1
            for k, q in enumerate(dirs):
                cx, cy, cz = VELOCITIES[q]
                spot = 32 * k if k < 3 else 32 * (k - 3)
                rows = zr[t, side, 0:8] if k < 3 else zr[t, side, 8:16]
                halo = pltpu.roll(rows, lax.rem(NL + edge - spot - p, NL), 1)
                incoming = jnp.where(lane == edge, halo, roll_z[CROSS.index(q), p + 1 - cx])
                incoming = shift_rows(incoming, cy)
                beside = fz[1 - cz, p + 1 - cx, 8 - cy : 16 - cy]
                empty = beside == 0.0
                back = f[opposite(q), p + 1]
                pair = q if q % 2 else q - 1
                got[q] = jnp.where(empty, eqs[Z_PAIRS.index(pair), p] - back, incoming)
                term = jnp.where(empty, 0.0, (fill + beside) * (incoming - back))
                ex = term if ex is None else ex + term
        diffs = {q: got[q] - got[q + 1] for q in Z_PAIRS}
        sums = {q: got[q] + got[q + 1] for q in Z_PAIRS}
        (mx, my, mz), total = moments(diffs, sums)
        dens = jnp.where(gas, 1.0, total + part[0, p])
        inv = 1.0 / dens
        vx, vy, vz = (mx + part[1, p]) * inv, (my + part[2, p]) * inv, mz * inv
        mass = part[3, p] + 0.5 * ex
        fill_new = jnp.where(kind == 2, 1.0, jnp.where(gas, 0.0, jnp.clip(mass * inv, 0.01, 1.0)))
        return got, dens, (vx, vy, vz), fill_new

    def collide(got, gas, dens, vx, vy, vz):
        wz = vz + RELAX_TIME * GRAVITY
        base = 1.0 - 1.5 * (vx * vx + vy * vy + wz * wz)
        keep = jnp.where(gas, 0.0, 1.0 - 1.0 / RELAX_TIME)
        scale = jnp.where(gas, 0.0, dens * (1.0 / RELAX_TIME))
        new = {0: keep * got[0] + (WEIGHTS[0] * scale) * base}
        by_weight = {w: (w * scale, 3.0 * w * scale) for w in (WEIGHTS[1], WEIGHTS[7])}
        for q in range(1, 19, 2):
            along = None
            for c, v in zip(VELOCITIES[q], (vx, vy, wz)):
                if c:
                    along = (v if c > 0 else -v) if along is None else (along + v if c > 0 else along - v)
            even_w, odd_w = by_weight[WEIGHTS[q]]
            even = even_w * (base + 4.5 * along * along)
            odd = odd_w * along
            new[q] = keep * got[q] + (even + odd)
            new[q + 1] = keep * got[q + 1] + (even - odd)
        return new

    def before_z(t, f, fz, sends):
        body = local_part(f, fz)

        def inner(p, c):
            body(p)
            return c

        lax.fori_loop(1, NP - 1, inner, 0, unroll=2)
        for c in sends[6:]:
            c.wait_recv()
        arrive_x(t, f, fz)

        def outer(i, c):
            body(i * (NP - 1))
            return c

        lax.fori_loop(0, 2, outer, 0, unroll=2)

    before_z(0, f0, fz0, pending)
    for c in pending[:6]:
        c.wait_recv()
    arrive_z(0, fz0)

    def first(p, acc):
        got, dens, (vx, vy, vz), fill_new = cross_part(0, f0, fz0, p)
        got[0] = f0[0, p + 1]
        for q in FLAT:
            got[q] = g_s[q, p]
        new = collide(got, flags[p] == 0, dens, vx, vy, vz)
        for q in range(19):
            f1[q, p + 1] = new[q]
        fz1[1, p + 1, 8:16] = fill_new
        return pack_columns([new[q] for q in UP], [new[q] for q in DOWN], fill_new, p, acc, lane)

    store_z(1, lax.fori_loop(0, NP, first, acc0, unroll=2))
    fill_x(1, f1, fz1)
    again = z_sends(1) + x_sends(1)
    for c in again:
        c.start()

    own.wait()
    pltpu.make_async_copy(heat_pad.at[0, pl.ds(1, ND - 1), pl.ds(8, 8)], heat_pad.at[0, pl.ds(1, ND - 1), pl.ds(8, 8)], hot_sem.at[1]).wait()

    def heat_columns(p, acc):
        h = heat_pad[0, p + 1, 8:16]
        here = lane == p
        return jnp.where(here, spread(h, NL - 1), acc[0]), jnp.where(here, spread(h, 0), acc[1])

    hcols = lax.fori_loop(0, NP, heat_columns, (zero8, zero8), unroll=8)
    hzs[0] = hcols[0]
    hzs[1] = hcols[1]

    def hsend(src, dst, n, to):
        return pltpu.make_async_remote_copy(
            src_ref=src, dst_ref=dst, send_sem=hsend_sem.at[n], recv_sem=hrecv_sem.at[n],
            device_id=to, device_id_type=MESH,
        )

    hs = [
        hsend(hzs.at[0], hzr.at[0], 0, (g, up)),
        hsend(hzs.at[1], hzr.at[1], 1, (g, down)),
        hsend(heat_pad.at[0, NP, pl.ds(8, 8)], hx.at[0], 2, (east, d)),
        hsend(heat_pad.at[0, 1, pl.ds(8, 8)], hx.at[1], 3, (west, d)),
    ]
    for c in hs:
        c.start()

    before_z(1, f1, fz1, again)

    for c in hs:
        c.wait_recv()
    heat_pad[0, 0, 8:16] = jnp.where(g > 0, hx[0], 0.0)
    heat_pad[0, NP + 1, 8:16] = jnp.where(g < NG - 1, hx[1], 0.0)
    hz_low = jnp.where(d > 0, hzr[0], 0.0)
    hz_high = jnp.where(d < ND - 1, hzr[1], 0.0)

    def temp(h):
        return jnp.minimum(h, 1.0) + jnp.maximum(h - 1.5, 0.0)

    def differences(p, c):
        h = heat_pad[0, p + 1, 8:16]
        low = jnp.where(lane == 0, pltpu.roll(hz_low, lax.rem(NL - p, NL), 1), pltpu.roll(h, 1, 1))
        high = jnp.where(lane == NL - 1, pltpu.roll(hz_high, NL - 1 - p, 1), pltpu.roll(h, NL - 1, 1))
        others = (
            heat_pad[0, p, 8:16], heat_pad[0, p + 2, 8:16],
            heat_pad[0, p + 1, 7:15], heat_pad[0, p + 1, 9:17],
            low, high,
        )
        mine = temp(h)
        total = None
        for k, other in enumerate(others):
            dt = temp(other) - mine
            total = dt if total is None else total + dt
            heat_d[k, p] = dt * (0.05 * STEP_TIME)
            heat_d[6 + k, p] = (other - h) * STEP_TIME
        heat_d[12, p] = total * STEP_TIME
        return c

    lax.fori_loop(0, NP, differences, 0, unroll=4)

    for c in again[:6]:
        c.wait_recv()
    arrive_z(1, fz1)

    def second(p, c):
        got, dens, v, fill_new = cross_part(1, f1, fz1, p)
        for q in CROSS:
            g_s[q, p] = got[q]
        vel[0, p] = dens
        for a in range(3):
            vel[1 + a, p] = v[a]
        fz2[1, p + 1, 8:16] = fill_new
        return c

    lax.fori_loop(0, NP, second, 0, unroll=2)

    xs[2, 0, 0] = fz2[1, NP, 8:16]
    xs[2, 1, 0] = fz2[1, 1, 8:16]
    last = [
        send(2, xs.at[2, 0, 0], xr.at[2, 0, 0], 0, (east, d)),
        send(2, xs.at[2, 1, 0], xr.at[2, 1, 0], 1, (west, d)),
    ]
    for c in last:
        c.start()
    fill_copy = pltpu.make_async_copy(fz2.at[1, pl.ds(1, NP), pl.ds(8, 8)], fill_out, out_sem.at[0])
    fill_copy.start()
    for c in last:
        c.wait_recv()
    fz2[1, 0, 8:16] = jnp.where(g > 0, xr[2, 0, 0], 0.0)
    fz2[1, NP + 1, 8:16] = jnp.where(g < NG - 1, xr[2, 1, 0], 0.0)

    def back_copy(p):
        return pltpu.make_async_remote_copy(
            src_ref=msg.at[p], dst_ref=warm_out.at[d],
            send_sem=aout_sem.at[0], recv_sem=aout_sem.at[1], device_id=(g, p), device_id_type=MESH,
        )

    def transport(i, c):
        p = lax.rem(d + i, ND)
        fill = fz2[1, p + 1, 8:16]
        beside = (
            fz2[1, p, 8:16], fz2[1, p + 2, 8:16], fz2[1, p + 1, 7:15], fz2[1, p + 1, 9:17],
            jnp.where(lane == 0, 0.0, pltpu.roll(fill, 1, 1)),
            jnp.where(lane == NL - 1, 0.0, pltpu.roll(fill, NL - 1, 1)),
        )
        out = heat_pad[0, p + 1, 8:16] + (0.02 + 0.05 * fill) * heat_d[12, p]
        for k in range(6):
            out = out + beside[k] * heat_d[k, p]
        for a in range(3):
            v = vel[1 + a, p]
            out = out + jnp.maximum(v, 0.0) * heat_d[6 + 2 * a, p] - jnp.minimum(v, 0.0) * heat_d[7 + 2 * a, p]
        msg[p, 0:8] = out
        msg[p, 8:16] = fill

        @pl.when(i < ND)
        def _():
            back_copy(p).start()

        return c

    lax.fori_loop(1, ND + 1, transport, 0)
    keep = pltpu.make_async_copy(msg.at[d], warm_out.at[d], load_sem.at[3])
    keep.start()

    def collide_again(p, c):
        got = {q: g_s[q, p] for q in FLAT + CROSS}
        got[0] = f1[0, p + 1]
        new = collide(got, flags[p] == 0, vel[0, p], vel[1, p], vel[2, p], vel[3, p])
        for q in range(19):
            f0[q, p + 1] = new[q]
        return c

    lax.fori_loop(0, NP, collide_again, 0, unroll=2)
    pops_copy = pltpu.make_async_copy(f0.at[:, pl.ds(1, NP)], pops_out, out_sem.at[1])
    pops_copy.start()

    for c in pending + again + hs + last:
        c.wait_send()
    pltpu.make_async_copy(heat_pad.at[0, pl.ds(1, ND - 1), pl.ds(8, 8)], heat_pad.at[0, pl.ds(1, ND - 1), pl.ds(8, 8)], hot_sem.at[0]).wait()
    keep.wait()
    fill_copy.wait()
    pops_copy.wait()
    pltpu.make_async_copy(msg.at[pl.ds(0, ND - 1)], msg.at[pl.ds(0, ND - 1)], aout_sem.at[0]).wait()
    pltpu.make_async_copy(msg.at[pl.ds(0, ND - 1)], msg.at[pl.ds(0, ND - 1)], aout_sem.at[1]).wait()


def finish_kernel(pops_mid, fill_mid, warm_mid, energy_in, pops_out, fill_out, energy_out, got, own, done, sem):
    copies = [
        pltpu.make_async_copy(warm_mid, got, sem.at[0]),
        pltpu.make_async_copy(energy_in, own, sem.at[1]),
        pltpu.make_async_copy(fill_mid, fill_out, sem.at[2]),
        pltpu.make_async_copy(pops_mid, pops_out, sem.at[3]),
    ]
    for c in copies:
        c.start()
    copies[0].wait()
    copies[1].wait()
    lane = lane_iota()

    def temp(h):
        return jnp.minimum(h, 1.0) + jnp.maximum(h - 1.5, 0.0)

    for e in range(ND):
        cells = slice(e * NL, (e + 1) * NL)
        out = got[e, 0:8]
        warmth = temp(own[0, :, cells])
        for side, other in ((0, e - 1), (1, e + 1)):
            if other < 0 or other >= ND:
                continue
            by, edge = (1, 0) if side == 0 else (NL - 1, NL - 1)
            beyond = temp(own[0, :, other * NL : (other + 1) * NL])
            term = pltpu.roll(got[other, 8:16], by, 1) * (pltpu.roll(beyond, by, 1) - warmth)
            out = out + jnp.where(lane == edge, (0.05 * STEP_TIME) * term, 0.0)
        done[0, :, cells] = out
    last = pltpu.make_async_copy(done, energy_out, sem.at[0])
    last.start()
    last.wait()
    copies[2].wait()
    copies[3].wait()


def shards(populations, fill, flags, specific_energy_grid):
    plane = (NY, NL)
    any_spec = pl.BlockSpec(memory_space=pl.ANY)
    pops_mid, fill_mid, warm_mid = pl.pallas_call(
        fluid_kernel,
        out_shape=(
            jax.ShapeDtypeStruct((19, NP) + plane, F32),
            jax.ShapeDtypeStruct((NP,) + plane, F32),
            jax.ShapeDtypeStruct((ND, 16, NL), F32),
        ),
        in_specs=[any_spec] * 4,
        out_specs=(any_spec,) * 3,
        scratch_shapes=[
            pltpu.VMEM((19, NP + 2) + plane, F32),
            pltpu.VMEM((19, NP + 2) + plane, F32),
            pltpu.VMEM((3, NP + 2, 24, NL), F32),
            pltpu.VMEM((3, NP + 2, 24, NL), F32),
            pltpu.VMEM((3, NP + 2, 24, NL), F32),
            pltpu.VMEM((10, NP + 2) + plane, F32),
            pltpu.VMEM((19, NP) + plane, F32),
            pltpu.VMEM((4, NP) + plane, F32),
            pltpu.VMEM((5, NP) + plane, F32),
            pltpu.VMEM((NP,) + plane, jnp.int32),
            pltpu.VMEM((4, NP) + plane, F32),
            pltpu.VMEM((2, NP + 2, 24, NL), F32),
            pltpu.VMEM((13, NP) + plane, F32),
            pltpu.VMEM((3, 2, 6) + plane, F32),
            pltpu.VMEM((3, 2, 6) + plane, F32),
            pltpu.VMEM((2, 2, 16, NL), F32),
            pltpu.VMEM((2, 2, 16, NL), F32),
            pltpu.VMEM((2, 2, 2, 16, NL), F32),
            pltpu.VMEM((2,) + plane, F32),
            pltpu.VMEM((2,) + plane, F32),
            pltpu.VMEM((2,) + plane, F32),
            pltpu.VMEM((ND, 16, NL), F32),
            pltpu.SemaphoreType.DMA((4,)),
            pltpu.SemaphoreType.DMA((3, 8)),
            pltpu.SemaphoreType.DMA((3, 8)),
            pltpu.SemaphoreType.DMA((2,)),
            pltpu.SemaphoreType.DMA((4,)),
            pltpu.SemaphoreType.DMA((4,)),
            pltpu.SemaphoreType.DMA((2,)),
            pltpu.SemaphoreType.DMA((2,)),
        ],
        compiler_params=pltpu.CompilerParams(
            collective_id=0, has_side_effects=True, vmem_limit_bytes=40 * 1024 * 1024
        ),
        name="pour",
    )(populations, fill, flags, specific_energy_grid)
    return pl.pallas_call(
        finish_kernel,
        out_shape=(
            jax.ShapeDtypeStruct((19, NP) + plane, F32),
            jax.ShapeDtypeStruct((NP,) + plane, F32),
            jax.ShapeDtypeStruct((1, NY, ND * NL), F32),
        ),
        in_specs=[any_spec] * 4,
        out_specs=(any_spec,) * 3,
        scratch_shapes=[
            pltpu.VMEM((ND, 16, NL), F32),
            pltpu.VMEM((1, NY, ND * NL), F32),
            pltpu.VMEM((1, NY, ND * NL), F32),
            pltpu.SemaphoreType.DMA((4,)),
        ],
        compiler_params=pltpu.CompilerParams(vmem_limit_bytes=8 * 1024 * 1024),
        name="finish",
    )(pops_mid, fill_mid, warm_mid, specific_energy_grid)


def solution(mesh):
    in_specs = (
        P(None, "grp", None, "dev"),
        P("grp", None, "dev"),
        P("grp", None, "dev"),
        P(("grp", "dev"), None, None),
    )
    out_specs = (P(None, "grp", None, "dev"), P("grp", None, "dev"), P(("grp", "dev"), None, None))
    return jax.shard_map(shards, mesh=mesh, in_specs=in_specs, out_specs=out_specs, check_vma=False)
```

profile of v0, /device:TPU:1, one launch (start us, length us, event | category | flops | bytes accessed | tf_op | source)
XLA Modules:
  0.0 40.8 jit_solution(3669506766691051637)
XLA Ops:
  0.6 0.0 copy-start
  0.6 1.7 %copy-done = f32[19,32,8,128]{3,2,1,0:T(8,128)S(1)} copy-done((f32[19,32,8,128]{3,2,1,0:T(8,128)S(1)}, f32[19,32,8,128]{3,2,1,0:T(8,128)}, u32[]{:S(2)}) %copy-start) | copy-done | bytes 2490392
  2.3 0.0 copy-start.1
  2.3 0.9 %copy-done.1 = f32[1,8,4096]{2,1,0:T(8,128)S(1)} copy-done((f32[1,8,4096]{2,1,0:T(8,128)S(1)}, f32[1,8,4096]{2,1,0:T(8,128)}, u32[]{:S(2)}) %copy-start.1) | copy-done | bytes 131096
  3.2 0.0 copy-start.2
  3.2 0.9 %copy-done.2 = f32[32,8,128]{2,1,0:T(8,128)S(1)} copy-done((f32[32,8,128]{2,1,0:T(8,128)S(1)}, f32[32,8,128]{2,1,0:T(8,128)}, u32[]{:S(2)}) %copy-start.2) | copy-done | bytes 131096
  4.1 0.0 copy-start.3
  4.1 0.9 %copy-done.3 = s32[32,8,128]{2,1,0:T(8,128)S(1)} copy-done((s32[32,8,128]{2,1,0:T(8,128)S(1)}, s32[32,8,128]{2,1,0:T(8,128)}, u32[]{:S(2)}) %copy-start.3) | copy-done | bytes 131096
  5.0 34.0 %pour.1 = (f32[19,32,8,128]{3,2,1,0:T(8,128)S(1)}, f32[32,8,128]{2,1,0:T(8,128)S(1)}, f32[32,16,128]{2,1,0:T(8,128)S(1)}) custom-call(f32[19,32,8,128]{3,2,1,0:T(8,128)S(1)} %copy-done, f32[32,8,128]{2,1,0:T(8,128)S(1)} %copy-done.2, s32[32,8,128]{2,1,0:T(8,128)S(1)} %copy-done.3, f32[1,8,4096]{2,1,0:T(8,128)S(1)} %copy-done.1), custom_call_target="tpu_custom_call" | custom-call | tf_op jit(solution)/shard_map/pour/pallas_call | solution.py:573
  39.1 1.7 %finish.1 = (f32[19,32,8,128]{3,2,1,0:T(8,128)}, f32[32,8,128]{2,1,0:T(8,128)}, f32[1,8,4096]{2,1,0:T(8,128)}) custom-call(f32[19,32,8,128]{3,2,1,0:T(8,128)S(1)} %get-tuple-element.6.pops_mid, f32[32,8,128]{2,1,0:T(8,128)S(1)} %get-tuple-element.7.fill_mid, f32[32,16,128]{2,1,0:T(8,128)S(1)} %get-tuple-element.8.warm_mid, f32[1,8,4096]{2,1,0:T(8,128)S(1)} %copy-done.1), custom_call_target="tpu_custom_call" | custom-call | tf_op jit(solution)/shard_map/finish/pallas_call | solution.py:619
Async XLA Ops:
  0.6 1.7 %copy-start = (f32[19,32,8,128]{3,2,1,0:T(8,128)S(1)}, f32[19,32,8,128]{3,2,1,0:T(8,128)}, u32[]{:S(2)}) copy-start(f32[19,32,8,128]{3,2,1,0:T(8,128)} %pops_in.1) | copy-start | bytes 7471108
  2.3 0.9 %copy-start.1 = (f32[1,8,4096]{2,1,0:T(8,128)S(1)}, f32[1,8,4096]{2,1,0:T(8,128)}, u32[]{:S(2)}) copy-start(f32[1,8,4096]{2,1,0:T(8,128)} %energy_in.3) | copy-start | bytes 393220
  3.2 0.9 %copy-start.2 = (f32[32,8,128]{2,1,0:T(8,128)S(1)}, f32[32,8,128]{2,1,0:T(8,128)}, u32[]{:S(2)}) copy-start(f32[32,8,128]{2,1,0:T(8,128)} %fill_in.1) | copy-start | bytes 393220
  4.1 0.9 %copy-start.3 = (s32[32,8,128]{2,1,0:T(8,128)S(1)}, s32[32,8,128]{2,1,0:T(8,128)}, u32[]{:S(2)}) copy-start(s32[32,8,128]{2,1,0:T(8,128)} %flags_in.1) | copy-start | bytes 393220
where the time goes:
time: 41 us; the launch traced here: 40.8 us
  Pallas kernels  35.8 us (87%)
  local copies, waits for them, and re-layouts  4.41 us (11%)
  between operations  0.65 us (2%)
    pallas_call x1, Pallas kernels, shards(): pl.pallas_call(fluid_kernel, out_shape=(jax.ShapeDtypeStruct((19, NP) + p...  34 us
    unnamed x8, local copies, waits for them, and re-layouts  4.41 us
    pallas_call x1, Pallas kernels, shards(): pl.pallas_call(finish_kernel, out_shape=(jax.ShapeDtypeStruct((19, NP) +...  1.74 us

commit v1 on v0

--- a/solution.py
+++ b/solution.py
@@ -150,6 +150,16 @@
             device_id=to, device_id_type=MESH,
         )
 
+    def ends_first(body, carry, between):
+        def block(base, c):
+            for j in range(4):
+                c = body(base + j, c)
+            return c
+
+        carry = lax.fori_loop(0, 2, lambda i, c: block(i * (NP - 4), c), carry)
+        between()
+        return lax.fori_loop(1, NP // 4 - 1, lambda i, c: block(i * 4, c), carry)
+
     def x_sends(t):
         return [
             send(t, xs.at[t, 0], xr.at[t, 0], 0, (east, d)),
@@ -185,7 +195,7 @@
         )
 
     acc0 = (zero8,) * 4
-    store_z(0, lax.fori_loop(0, NP, pack0, acc0, unroll=4))
+    store_z(0, lax.fori_loop(0, NP, pack0, acc0, unroll=8))
 
     pl.semaphore_wait(barrier, 37)
     pending = z_sends(0) + x_sends(0)
@@ -236,6 +246,8 @@
                 eqs[k, p] = paired(q)
             for k, q in enumerate(CROSS):
                 roll_z[k, p + 1] = pltpu.roll(pops[q], 1 if q in UP else NL - 1, 1)
+            fz[0, p + 1, 8:16] = pltpu.roll(fill, 1, 1)
+            fz[2, p + 1, 8:16] = pltpu.roll(fill, NL - 1, 1)
             ex = None
             got = {0: pops[0]}
             for q in FLAT:
@@ -272,28 +284,27 @@
             roll_z[CROSS.index(q), NP + 1] = pltpu.roll(f[q, NP + 1], 1 if q in UP else NL - 1, 1)
 
     def arrive_z(t, fz):
+        inside = (d > 0, d < ND - 1)
+        fills = []
         for side in range(2):
-            inside = d > 0 if side == 0 else d < ND - 1
-            main0, main1 = zr[t, side, 0:8], zr[t, side, 8:16]
-            b = jnp.where(lane == 0, zd[t, side, 0, 8:16], main1)
+            b = jnp.where(lane == 0, zd[t, side, 0, 8:16], zr[t, side, 8:16])
             b = jnp.where(lane == 63, zd[t, side, 1, 8:16], b)
             zr[t, side, 8:16] = b
-            edge = 0 if side == 0 else NL - 1
-            k = 0 if side == 0 else 2
-            by = 1 if side == 0 else NL - 1
-
-            def column(p, c):
-                old = pltpu.roll(fz[1, p + 1, 8:16], by, 1)
-                new = pltpu.roll(main0, lax.rem(NL + edge - 96 - p, NL), 1)
-                fz[k, p + 1, 8:16] = jnp.where(lane == edge, jnp.where(inside, new, 0.0), old)
-                return c
-
-            lax.fori_loop(0, NP, column, 0, unroll=8)
+            fills.append(jnp.where(inside[side], zr[t, side, 0:8], 0.0))
+            edge, k, by = ((0, 0, 1), (NL - 1, 2, NL - 1))[side]
             for at, src, spot, ok in ((0, 0, 127, g > 0), (NP + 1, 1, 96, g < NG - 1)):
                 old = pltpu.roll(fz[1, at, 8:16], by, 1)
                 new = spread(zd[t, side, src, 0:8], spot)
-                ok = jnp.logical_and(ok, inside)
+                ok = jnp.logical_and(ok, inside[side])
                 fz[k, at, 8:16] = jnp.where(lane == edge, jnp.where(ok, new, 0.0), old)
+
+        def column(p, c):
+            for side, edge, k in ((0, 0, 0), (1, NL - 1, 2)):
+                new = pltpu.roll(fills[side], lax.rem(NL + edge - 96 - p, NL), 1)
+                fz[k, p + 1, 8:16] = jnp.where(lane == edge, new, fz[k, p + 1, 8:16])
+            return c
+
+        lax.fori_loop(0, NP, column, 0, unroll=16)
 
     def cross_part(t, f, fz, p):
         kind = flags[p]
@@ -353,7 +364,7 @@
             body(p)
             return c
 
-        lax.fori_loop(1, NP - 1, inner, 0, unroll=2)
+        lax.fori_loop(1, NP - 1, inner, 0, unroll=5)
         for c in sends[6:]:
             c.wait_recv()
         arrive_x(t, f, fz)
@@ -380,10 +391,15 @@
         fz1[1, p + 1, 8:16] = fill_new
         return pack_columns([new[q] for q in UP], [new[q] for q in DOWN], fill_new, p, acc, lane)
 
-    store_z(1, lax.fori_loop(0, NP, first, acc0, unroll=2))
-    fill_x(1, f1, fz1)
     again = z_sends(1) + x_sends(1)
-    for c in again:
+
+    def first_ends():
+        fill_x(1, f1, fz1)
+        for c in again[6:]:
+            c.start()
+
+    store_z(1, ends_first(first, acc0, first_ends))
+    for c in again[:6]:
         c.start()
 
     own.wait()
@@ -444,7 +460,7 @@
         heat_d[12, p] = total * STEP_TIME
         return c
 
-    lax.fori_loop(0, NP, differences, 0, unroll=4)
+    lax.fori_loop(0, NP, differences, 0, unroll=8)
 
     for c in again[:6]:
         c.wait_recv()
@@ -460,16 +476,18 @@
         fz2[1, p + 1, 8:16] = fill_new
         return c
 
-    lax.fori_loop(0, NP, second, 0, unroll=2)
-
-    xs[2, 0, 0] = fz2[1, NP, 8:16]
-    xs[2, 1, 0] = fz2[1, 1, 8:16]
     last = [
         send(2, xs.at[2, 0, 0], xr.at[2, 0, 0], 0, (east, d)),
         send(2, xs.at[2, 1, 0], xr.at[2, 1, 0], 1, (west, d)),
     ]
-    for c in last:
-        c.start()
+
+    def second_ends():
+        xs[2, 0, 0] = fz2[1, NP, 8:16]
+        xs[2, 1, 0] = fz2[1, 1, 8:16]
+        for c in last:
+            c.start()
+
+    ends_first(second, 0, second_ends)
     fill_copy = pltpu.make_async_copy(fz2.at[1, pl.ds(1, NP), pl.ds(8, 8)], fill_out, out_sem.at[0])
     fill_copy.start()
     for c in last:
@@ -483,8 +501,7 @@
             send_sem=aout_sem.at[0], recv_sem=aout_sem.at[1], device_id=(g, p), device_id_type=MESH,
         )
 
-    def transport(i, c):
-        p = lax.rem(d + i, ND)
+    def transport(p, c):
         fill = fz2[1, p + 1, 8:16]
         beside = (
             fz2[1, p, 8:16], fz2[1, p + 2, 8:16], fz2[1, p + 1, 7:15], fz2[1, p + 1, 9:17],
@@ -499,14 +516,15 @@
             out = out + jnp.maximum(v, 0.0) * heat_d[6 + 2 * a, p] - jnp.minimum(v, 0.0) * heat_d[7 + 2 * a, p]
         msg[p, 0:8] = out
         msg[p, 8:16] = fill
-
-        @pl.when(i < ND)
-        def _():
-            back_copy(p).start()
-
-        return c
-
-    lax.fori_loop(1, ND + 1, transport, 0)
+        return c
+
+    lax.fori_loop(0, NP, transport, 0, unroll=8)
+
+    def back_start(i, c):
+        back_copy(lax.rem(d + i, ND)).start()
+        return c
+
+    lax.fori_loop(1, ND, back_start, 0)
     keep = pltpu.make_async_copy(msg.at[d], warm_out.at[d], load_sem.at[3])
     keep.start()
 
@@ -570,6 +588,11 @@
 def shards(populations, fill, flags, specific_energy_grid):
     plane = (NY, NL)
     any_spec = pl.BlockSpec(memory_space=pl.ANY)
+    hbm_spec = pl.BlockSpec(memory_space=pltpu.HBM)
+    given = [
+        pltpu.with_memory_space_constraint(x, pltpu.HBM)
+        for x in (populations, fill, flags, specific_energy_grid)
+    ]
     pops_mid, fill_mid, warm_mid = pl.pallas_call(
         fluid_kernel,
         out_shape=(
@@ -577,7 +600,7 @@
             jax.ShapeDtypeStruct((NP,) + plane, F32),
             jax.ShapeDtypeStruct((ND, 16, NL), F32),
         ),
-        in_specs=[any_spec] * 4,
+        in_specs=[hbm_spec] * 4,
         out_specs=(any_spec,) * 3,
         scratch_shapes=[
             pltpu.VMEM((19, NP + 2) + plane, F32),
@@ -615,7 +638,7 @@
             collective_id=0, has_side_effects=True, vmem_limit_bytes=40 * 1024 * 1024
         ),
         name="pour",
-    )(populations, fill, flags, specific_energy_grid)
+    )(*given)
     return pl.pallas_call(
         finish_kernel,
         out_shape=(
@@ -633,7 +656,7 @@
         ],
         compiler_params=pltpu.CompilerParams(vmem_limit_bytes=8 * 1024 * 1024),
         name="finish",
-    )(pops_mid, fill_mid, warm_mid, specific_energy_grid)
+    )(pops_mid, fill_mid, warm_mid, given[3])
 
 
 def solution(mesh):

time: 41 us -> 32.4 us (0.79)
  local copies, waits for them, and re-layouts: 4.41 us -> 0 us
  Pallas kernels: 35.8 us -> 31.6 us
    unnamed x8 -> x0, local copies, waits for them, and re-layouts: 4.41 us -> none
    pallas_call x1, Pallas kernels: 34 us -> 29.7 us  [shards(): pl.pallas_call(fluid_kernel, out_shape=(jax.ShapeDtypeStruct((19, NP) + p...]
where the time goes in v1:
time: 32.4 us; the launch traced here: 32.3 us
  Pallas kernels  31.6 us (98%)
  between operations  0.64 us (2%)
    pallas_call x1, Pallas kernels, shards(): pl.pallas_call(fluid_kernel, out_shape=(jax.ShapeDtypeStruct((19, NP) + p...  29.7 us
    pallas_call x1, Pallas kernels, shards(): pl.pallas_call(finish_kernel, out_shape=(jax.ShapeDtypeStruct((19, NP) +...  1.94 us

profile of v1, /device:TPU:1, one launch (start us, length us, event | category | flops | bytes accessed | tf_op | source)
XLA Modules:
  0.0 32.3 jit_solution(12316147399917622911)
XLA Ops:
  0.6 29.7 %pour.1 = (f32[19,32,8,128]{3,2,1,0:T(8,128)S(1)}, f32[32,8,128]{2,1,0:T(8,128)S(1)}, f32[32,16,128]{2,1,0:T(8,128)S(1)}) custom-call(f32[19,32,8,128]{3,2,1,0:T(8,128)} %pops_in.1, f32[32,8,128]{2,1,0:T(8,128)} %fill_in.1, s32[32,8,128]{2,1,0:T(8,128)} %flags_in.1, f32[1,8,4096]{2,1,0:T(8,128)} %energy_in.3), custom_call_target="tpu_custom_call" | custom-call | tf_op jit(solution)/shard_map/pour/pallas_call | solution.py:596
  30.3 1.9 %finish.1 = (f32[19,32,8,128]{3,2,1,0:T(8,128)}, f32[32,8,128]{2,1,0:T(8,128)}, f32[1,8,4096]{2,1,0:T(8,128)}) custom-call(f32[19,32,8,128]{3,2,1,0:T(8,128)S(1)} %get-tuple-element.6.pops_mid, f32[32,8,128]{2,1,0:T(8,128)S(1)} %get-tuple-element.7.fill_mid, f32[32,16,128]{2,1,0:T(8,128)S(1)} %get-tuple-element.8.warm_mid, f32[1,8,4096]{2,1,0:T(8,128)} %energy_in.3), custom_call_target="tpu_custom_call" | custom-call | tf_op jit(solution)/shard_map/finish/pallas_call | solution.py:642

commit v2 on v1

v2 whole, which is shorter than its diff:
```python
import functools

import jax
import jax.numpy as jnp
from jax import lax
from jax.experimental import pallas as pl
from jax.experimental.pallas import tpu as pltpu
from jax.sharding import PartitionSpec as P

MESH = pl.DeviceIdType.MESH
F32 = jnp.float32
VELOCITIES = (
    (0, 0, 0),
    (1, 0, 0),
    (-1, 0, 0),
    (0, 1, 0),
    (0, -1, 0),
    (0, 0, 1),
    (0, 0, -1),
    (1, 1, 0),
    (-1, -1, 0),
    (1, -1, 0),
    (-1, 1, 0),
    (1, 0, 1),
    (-1, 0, -1),
    (1, 0, -1),
    (-1, 0, 1),
    (0, 1, 1),
    (0, -1, -1),
    (0, 1, -1),
    (0, -1, 1),
)
WEIGHTS = (1.0 / 3.0,) + (1.0 / 18.0,) * 6 + (1.0 / 36.0,) * 12
RELAX_TIME = 0.8
GRAVITY = -0.002
STEP_TIME = 0.2

NG, ND, NP, NY, NL = 4, 32, 32, 8, 128
FLAT = (1, 2, 3, 4, 7, 8, 9, 10)
UP = (5, 15, 18, 11, 14)
DOWN = (6, 16, 17, 13, 12)
CROSS = UP + DOWN
EAST = (1, 7, 9, 11, 13)
WEST = (2, 8, 10, 12, 14)
Z_PAIRS = (5, 11, 13, 15, 17)


FAR_FIRST = sorted(
    ((dz, dy, dc) for dz in range(4) for dy in range(4) for dc in range(2) if dz or dy or dc),
    key=lambda at: -(min(at[0], 4 - at[0]) + min(at[1], 4 - at[1])),
)


def opposite(q):
    return q + 1 if q % 2 == 1 else q - 1


def lane_iota():
    return lax.broadcasted_iota(jnp.int32, (NY, NL), 1)


def shift_rows(x, cy):
    return x if cy == 0 else pltpu.roll(x, cy % NY, 0)


def spread(x, lane):
    return jnp.broadcast_to(x[:, lane : lane + 1], (NY, NL))


def moments(d, s):
    out = []
    for axis in range(3):
        total = None
        for q, diff in d.items():
            c = VELOCITIES[q][axis]
            if c == 0:
                continue
            if total is None:
                total = diff if c > 0 else -diff
            else:
                total = total + diff if c > 0 else total - diff
        out.append(total)
    return out, sum(s.values())


def pack_columns(tops, bottoms, fill, p, acc, lane):
    spot = lane & 31
    here = spot == p
    east = lane == ((p + 1) & 31)
    west = lane == 32 + ((p + 31) & 31)
    out = []
    for side, (cols, edge) in enumerate(((tops, NL - 1), (bottoms, 0))):
        a, b = acc[2 * side], acc[2 * side + 1]
        v = spread(cols[0], edge)
        v = jnp.where(lane >= 32, spread(cols[1], edge), v)
        v = jnp.where(lane >= 64, spread(cols[2], edge), v)
        v = jnp.where(lane >= 96, spread(fill, edge), v)
        a = jnp.where(here, v, a)
        b = jnp.where(east, spread(cols[3], edge), b)
        b = jnp.where(west, spread(cols[4], edge), b)
        out += [a, b]
    return tuple(out)


def fluid_kernel(
    pops_in, fill_in, flags_in, energy_in,
    pops_out, fill_out, warm_out, ends_out,
    f0, f1, fz0, fz1, fz2, roll_z, halo_s, g_s, part, eqs, flags, vel, own_e, hot_msg, hbuf, heat_d,
    xs, xr, zs, zr, zd, msg, end_msg,
    load_sem, send_sem, recv_sem, hot_sem, back_sem, out_sem, group_sem, next_sem,
):
    g, d = lax.axis_index("grp"), lax.axis_index("dev")
    up, down = lax.rem(d + 1, ND), lax.rem(d + ND - 1, ND)
    east, west = lax.rem(g + 1, NG), lax.rem(g + NG - 1, NG)
    lane = lane_iota()
    row = lax.broadcasted_iota(jnp.int32, (NY, NL), 0)
    zero8 = jnp.zeros((NY, NL), F32)

    def load(src, dst, n):
        c = pltpu.make_async_copy(src, dst, load_sem.at[n])
        c.start()
        return c

    def load_pops(q, count, n):
        return load(pops_in.at[pl.ds(q, count)], f0.at[pl.ds(q, count), pl.ds(1, NP)], n)

    fill_load = load(fill_in, fz0.at[1, pl.ds(1, NP), pl.ds(8, 8)], 0)
    cross_loads = [load_pops(11, 8, 1), load_pops(5, 2, 2)]
    more_loads = [load_pops(0, 5, 3), load_pops(7, 4, 4), load(flags_in, flags, 5)]
    energy_load = load(energy_in.at[0], own_e.at[:, pl.ds(NL, ND * NL)], 6)

    z, y, core = lax.div(d, 8), lax.rem(lax.div(d, 2), 4), lax.rem(d, 2)
    barrier = pltpu.get_barrier_semaphore()
    column_peers = [(g, lax.rem(d + 8 * k, ND)) for k in range(1, 4)]
    x_peers = [(east, d), (west, d)]
    near = [(gg, dd) for dd in (up, down, d) for gg in (east, west)] + [(g, up), (g, down)]
    near += column_peers + [(g, 8 * z + lax.rem(d + k, 8)) for k in range(1, 8)]
    for to in near:
        pl.semaphore_signal(barrier, inc=1, device_id=to, device_id_type=MESH)

    def clear(p, c):
        for k in range(3):
            for ref in (fz0, fz1):
                ref[k, p, 0:8] = zero8
                ref[k, p, 16:24] = zero8
        fz2[p, 0:8] = zero8
        fz2[p, 16:24] = zero8
        return c

    lax.fori_loop(0, NP + 2, clear, 0)
    fz2[0, 8:16] = zero8
    fz2[NP + 1, 8:16] = zero8
    own_e[:, 0:NL] = zero8
    own_e[:, (ND + 1) * NL : (ND + 2) * NL] = zero8

    def send(t, src, dst, n, to):
        return pltpu.make_async_remote_copy(
            src_ref=src, dst_ref=dst, send_sem=send_sem.at[t, n], recv_sem=recv_sem.at[t, n],
            device_id=to, device_id_type=MESH,
        )

    def x_sends(t):
        return [
            send(t, xs.at[t, 0], xr.at[t, 0], 0, (east, d)),
            send(t, xs.at[t, 1], xr.at[t, 1], 1, (west, d)),
        ]

    def z_sends(t):
        return [
            send(t, zs.at[t, side], zr.at[t, side], 2 + side, (g, to))
            for side, to in ((0, up), (1, down))
        ]

    def corner_sends(t):
        return [
            send(t, zs.at[t, side], zd.at[t, side, k], 4 + 2 * side + k, (gg, to))
            for side, to in ((0, up), (1, down))
            for k, gg in ((0, east), (1, west))
        ]

    def fill_x(t, f, fz):
        for k, q in enumerate(EAST):
            xs[t, 0, k] = f[q, NP]
        xs[t, 0, 5] = fz[1, NP, 8:16]
        for k, q in enumerate(WEST):
            xs[t, 1, k] = f[q, 1]
        xs[t, 1, 5] = fz[1, 1, 8:16]

    def store_z(t, acc):
        for side in range(2):
            zs[t, side, 0:8] = acc[2 * side]
            zs[t, side, 8:16] = acc[2 * side + 1]

    def started(copies):
        for c in copies:
            c.start()
        return copies

    def arrived(copies):
        for c in copies:
            c.wait_recv()

    fill_load.wait()
    for c in cross_loads:
        c.wait()

    def pack0(p, acc):
        return pack_columns(
            [f0[q, p + 1] for q in UP], [f0[q, p + 1] for q in DOWN], fz0[1, p + 1, 8:16], p, acc, lane
        )

    acc0 = (zero8,) * 4
    store_z(0, lax.fori_loop(0, NP, pack0, acc0, unroll=8))

    pl.semaphore_wait(barrier, len(near))
    for to in column_peers:
        pl.semaphore_signal(group_sem, inc=1, device_id=to, device_id_type=MESH)

    corner0 = started(corner_sends(0))
    z0 = started(z_sends(0))
    for c in more_loads:
        c.wait()
    fill_x(0, f0, fz0)
    x0 = started(x_sends(0))

    def local_part(f, fz):
        def body(p):
            pops = [f[q, p + 1] for q in range(19)]
            kind = flags[p]
            gas = kind == 0
            fill = fz[1, p + 1, 8:16]
            diffs = {q: pops[q] - pops[q + 1] for q in range(1, 19, 2)}
            sums = {q: pops[q] + pops[q + 1] for q in range(1, 19, 2)}
            (mx, my, mz), total = moments(diffs, sums)
            dens = jnp.where(gas, 1.0, total + pops[0])
            inv = 1.0 / dens
            vx, vy, vz = mx * inv, my * inv, mz * inv
            base = 1.0 - 1.5 * (vx * vx + vy * vy + vz * vz)

            def paired(q):
                cx, cy, cz = VELOCITIES[q]
                along = None
                for c, v in ((cx, vx), (cy, vy), (cz, vz)):
                    if c:
                        along = (v if c > 0 else -v) if along is None else (along + v if c > 0 else along - v)
                return (2.0 * WEIGHTS[q]) * (base + 4.5 * along * along)

            for k, q in enumerate(Z_PAIRS):
                eqs[k, p] = paired(q)
            for k, q in enumerate(CROSS):
                roll_z[k, p + 1] = pltpu.roll(pops[q], 1 if q in UP else NL - 1, 1)
            fz[0, p + 1, 8:16] = pltpu.roll(fill, 1, 1)
            fz[2, p + 1, 8:16] = pltpu.roll(fill, NL - 1, 1)
            ex = None
            got = {0: pops[0]}
            for q in FLAT:
                cx, cy, _ = VELOCITIES[q]
                incoming = shift_rows(f[q, p + 1 - cx], cy)
                beside = fz[1, p + 1 - cx, 8 - cy : 16 - cy]
                empty = beside == 0.0
                back = pops[opposite(q)]
                got[q] = jnp.where(empty, paired(q if q % 2 else q - 1) - back, incoming)
                term = jnp.where(empty, 0.0, (fill + beside) * (incoming - back))
                ex = term if ex is None else ex + term
                g_s[q, p] = got[q]
            diffs = {q: got[q] - got[q + 1] for q in FLAT if q % 2}
            sums = {q: got[q] + got[q + 1] for q in FLAT if q % 2}
            (mx, my, _), total = moments(diffs, sums)
            part[0, p] = total + got[0]
            part[1, p] = mx
            part[2, p] = my
            part[3, p] = fill * dens + 0.5 * ex

        return body

    def local_inner(f, fz):
        body = local_part(f, fz)

        def inner(p, c):
            body(p)
            return c

        lax.fori_loop(1, NP - 1, inner, 0, unroll=6)

    def local_outer(t, f, fz):
        for k, q in enumerate(EAST):
            f[q, 0] = xr[t, 0, k]
        for k, q in enumerate(WEST):
            f[q, NP + 1] = xr[t, 1, k]
        fz[1, 0, 8:16] = jnp.where(g > 0, xr[t, 0, 5], 0.0)
        fz[1, NP + 1, 8:16] = jnp.where(g < NG - 1, xr[t, 1, 5], 0.0)
        for q in (11, 13):
            roll_z[CROSS.index(q), 0] = pltpu.roll(f[q, 0], 1 if q in UP else NL - 1, 1)
        for q in (12, 14):
            roll_z[CROSS.index(q), NP + 1] = pltpu.roll(f[q, NP + 1], 1 if q in UP else NL - 1, 1)
        body = local_part(f, fz)

        def outer(i, c):
            body(i * (NP - 1))
            return c

        lax.fori_loop(0, 2, outer, 0, unroll=2)

    def cross_part(f, fz, fill_ref, p):
        kind = flags[p]
        gas = kind == 0
        fill = fz[1, p + 1, 8:16]
        got = {}
        ex = None
        for side, dirs in enumerate((UP, DOWN)):
            edge = 0 if side == 0 else NL - 1
            for q in dirs:
                cx, cy, cz = VELOCITIES[q]
                k = CROSS.index(q)
                incoming = jnp.where(lane == edge, halo_s[k, p], roll_z[k, p + 1 - cx])
                incoming = shift_rows(incoming, cy)
                beside = fz[1 - cz, p + 1 - cx, 8 - cy : 16 - cy]
                empty = beside == 0.0
                back = f[opposite(q), p + 1]
                pair = q if q % 2 else q - 1
                got[q] = jnp.where(empty, eqs[Z_PAIRS.index(pair), p] - back, incoming)
                term = jnp.where(empty, 0.0, (fill + beside) * (incoming - back))
                ex = term if ex is None else ex + term
                g_s[q, p] = got[q]
        diffs = {q: got[q] - got[q + 1] for q in Z_PAIRS}
        sums = {q: got[q] + got[q + 1] for q in Z_PAIRS}
        (mx, my, mz), total = moments(diffs, sums)
        dens = jnp.where(gas, 1.0, total + part[0, p])
        inv = 1.0 / dens
        vel[0, p] = dens
        vel[1, p] = (mx + part[1, p]) * inv
        vel[2, p] = (my + part[2, p]) * inv
        vel[3, p] = mz * inv
        mass = part[3, p] + 0.5 * ex
        fill_ref[p + 1, 8:16] = jnp.where(
            kind == 2, 1.0, jnp.where(gas, 0.0, jnp.clip(mass * inv, 0.01, 1.0))
        )

    def cross(t, f, fz, fill_ref, corner):
        inside = (d > 0, d < ND - 1)
        fills = [jnp.where(inside[side], zr[t, side, 0:8], 0.0) for side in range(2)]

        def halos(p):
            for side, dirs in enumerate((UP, DOWN)):
                edge = 0 if side == 0 else NL - 1
                for k, q in enumerate(dirs):
                    spot = 32 * k if k < 3 else 32 * (k - 3)
                    rows = zr[t, side, 0:8] if k < 3 else zr[t, side, 8:16]
                    halo_s[CROSS.index(q), p] = pltpu.roll(rows, lax.rem(NL + edge - spot - p, NL), 1)

        def fill_columns(p):
            for side, edge, k in ((0, 0, 0), (1, NL - 1, 2)):
                new = pltpu.roll(fills[side], lax.rem(2 * NL + edge - 96 - p, NL), 1)
                fz[k, p + 1, 8:16] = jnp.where(lane == edge, new, fz[k, p + 1, 8:16])

        def prepare(base):
            for j in range(4):
                halos(base + j)
                fill_columns(base + j + 1)

        def work(base):
            for j in range(4):
                cross_part(f, fz, fill_ref, base + j)

        fill_columns(3)
        fill_columns(4)
        prepare(4)

        def mid(i, c):
            for base in (8 * i + 4, 8 * i + 8):
                work(base)
                prepare(base + 4)
            return c

        lax.fori_loop(0, NP // 8 - 1, mid, 0)

        arrived(corner)
        for side in range(2):
            b = jnp.where(lane == 0, zd[t, side, 0, 8:16], zr[t, side, 8:16])
            b = jnp.where(lane == 63, zd[t, side, 1, 8:16], b)
            zr[t, side, 8:16] = b
            edge, k, by = ((0, 0, 1), (NL - 1, 2, NL - 1))[side]
            for at, src, spot, ok in ((0, 0, 127, g > 0), (NP + 1, 1, 96, g < NG - 1)):
                old = pltpu.roll(fz[1, at, 8:16], by, 1)
                new = spread(zd[t, side, src, 0:8], spot)
                ok = jnp.logical_and(ok, inside[side])
                fz[k, at, 8:16] = jnp.where(lane == edge, jnp.where(ok, new, 0.0), old)
        for j in range(4):
            halos(j)
            halos(NP - 4 + j)
        for j in range(3):
            fill_columns(j)

        def last(i, c):
            work(i * (NP - 4))
            return c

        lax.fori_loop(0, 2, last, 0)

    def collide(f, p):
        gas = flags[p] == 0
        vx, vy, wz = vel[1, p], vel[2, p], vel[3, p] + RELAX_TIME * GRAVITY
        base = 1.0 - 1.5 * (vx * vx + vy * vy + wz * wz)
        keep = jnp.where(gas, 0.0, 1.0 - 1.0 / RELAX_TIME)
        scale = jnp.where(gas, 0.0, vel[0, p] * (1.0 / RELAX_TIME))
        new = {0: keep * f[0, p + 1] + (WEIGHTS[0] * scale) * base}
        by_weight = {w: (w * scale, 3.0 * w * scale) for w in (WEIGHTS[1], WEIGHTS[7])}
        for q in range(1, 19, 2):
            along = None
            for c, v in zip(VELOCITIES[q], (vx, vy, wz)):
                if c:
                    along = (v if c > 0 else -v) if along is None else (along + v if c > 0 else along - v)
            even_w, odd_w = by_weight[WEIGHTS[q]]
            even = even_w * (base + 4.5 * along * along)
            odd = odd_w * along
            new[q] = keep * g_s[q, p] + (even + odd)
            new[q + 1] = keep * g_s[q + 1, p] + (even - odd)
        return new

    local_inner(f0, fz0)

    energy_load.wait()

    def block_of(e):
        return own_e[:, pl.ds(pl.multiple_of((e + 1) * NL, NL), NL)]

    def hot_build(e, c):
        hot_msg[e, 0:8] = block_of(e)
        beside = jnp.where(lane == 0, pltpu.roll(block_of(e - 1), 1, 1), pltpu.roll(block_of(e + 1), NL - 1, 1))
        hot_msg[e, 8:16] = beside
        return c

    lax.fori_loop(0, ND, hot_build, 0, unroll=8)

    pl.semaphore_wait(group_sem, len(column_peers))
    for to in x_peers:
        pl.semaphore_signal(next_sem, inc=1, device_id=to, device_id_type=MESH)

    def hot_start(i, c):
        to = lax.rem(d + i, ND)
        pltpu.make_async_remote_copy(
            src_ref=hot_msg.at[to], dst_ref=hbuf.at[d + 1],
            send_sem=hot_sem.at[0], recv_sem=hot_sem.at[1], device_id=(g, to), device_id_type=MESH,
        ).start()
        return c

    lax.fori_loop(1, ND, hot_start, 0)
    own = pltpu.make_async_copy(hot_msg.at[d], hbuf.at[d + 1], load_sem.at[0])
    own.start()

    pl.semaphore_wait(next_sem, len(x_peers))

    def beyond(i, gg, at, sem):
        to = lax.rem(d + i, ND)
        return pltpu.make_async_remote_copy(
            src_ref=hot_msg.at[to, pl.ds(0, 8)], dst_ref=hbuf.at[at, pl.ds(0, 8)],
            send_sem=hot_sem.at[4], recv_sem=hot_sem.at[sem], device_id=(gg, to), device_id_type=MESH,
        )

    def beyond_all(gg, at, sem):
        def one(i, c):
            beyond(i, gg, at, sem).start()
            return c

        lax.fori_loop(0, ND, one, 0)

    @pl.when(d == ND - 1)
    def _():
        beyond_all(east, 0, 2)

    @pl.when(d == 0)
    def _():
        beyond_all(west, NP + 1, 3)

    arrived(x0)
    local_outer(0, f0, fz0)
    arrived(z0)
    cross(0, f0, fz0, fz1.at[1], corner0)

    def first(p, acc):
        new = collide(f0, p)
        for q in range(19):
            f1[q, p + 1] = new[q]
        return pack_columns([new[q] for q in UP], [new[q] for q in DOWN], fz1[1, p + 1, 8:16], p, acc, lane)

    store_z(1, lax.fori_loop(0, NP, first, acc0, unroll=8))
    corner1 = started(corner_sends(1))
    z1 = started(z_sends(1))
    fill_x(1, f1, fz1)
    x1 = started(x_sends(1))

    local_inner(f1, fz1)

    own.wait()
    pltpu.make_async_copy(hot_msg.at[pl.ds(0, ND - 1)], hot_msg.at[pl.ds(0, ND - 1)], hot_sem.at[1]).wait()
    beyond(0, east, 0, 2).wait_recv()
    beyond(0, west, NP + 1, 3).wait_recv()
    hbuf[0, 0:8] = jnp.where(g > 0, hbuf[0, 0:8], 0.0)
    hbuf[NP + 1, 0:8] = jnp.where(g < NG - 1, hbuf[NP + 1, 0:8], 0.0)

    def temp(h):
        return jnp.minimum(h, 1.0) + jnp.maximum(h - 1.5, 0.0)

    def differences(p, c):
        h = hbuf[p + 1, 0:8]
        edges = hbuf[p + 1, 8:16]
        others = (
            hbuf[p, 0:8], hbuf[p + 2, 0:8],
            jnp.where(row == 0, 0.0, pltpu.roll(h, 1, 0)), jnp.where(row == NY - 1, 0.0, pltpu.roll(h, NY - 1, 0)),
            jnp.where(lane == 0, edges, pltpu.roll(h, 1, 1)), jnp.where(lane == NL - 1, edges, pltpu.roll(h, NL - 1, 1)),
        )
        mine = temp(h)
        total = None
        for k, other in enumerate(others):
            dt = temp(other) - mine
            total = dt if total is None else total + dt
            heat_d[k, p] = dt * (0.05 * STEP_TIME)
            heat_d[6 + k, p] = (other - h) * STEP_TIME
        heat_d[12, p] = total * STEP_TIME
        return c

    lax.fori_loop(0, NP, differences, 0, unroll=8)

    arrived(x1)
    local_outer(1, f1, fz1)
    arrived(z1)
    cross(1, f1, fz1, fz2, corner1)

    end_msg[0] = -fz2[NP, 8:16] * heat_d[1, NP - 1]
    end_msg[1] = -fz2[1, 8:16] * heat_d[0, 0]
    end_sends = [
        pltpu.make_async_remote_copy(
            src_ref=end_msg.at[k], dst_ref=ends_out.at[k, d],
            send_sem=back_sem.at[2 + k], recv_sem=back_sem.at[4 + k], device_id=to, device_id_type=MESH,
        )
        for k, to in ((0, (east, 0)), (1, (west, ND - 1)))
    ]
    for c in end_sends:
        c.start()

    def transport(p, c):
        fill = fz2[p + 1, 8:16]
        beside = (
            fz2[p, 8:16], fz2[p + 2, 8:16], fz2[p + 1, 7:15], fz2[p + 1, 9:17],
            jnp.where(lane == 0, 0.0, pltpu.roll(fill, 1, 1)),
            jnp.where(lane == NL - 1, 0.0, pltpu.roll(fill, NL - 1, 1)),
        )
        out = hbuf[p + 1, 0:8] + (0.02 + 0.05 * fill) * heat_d[12, p]
        for k in range(6):
            out = out + beside[k] * heat_d[k, p]
        for a in range(3):
            v = vel[1 + a, p]
            out = out + jnp.maximum(v, 0.0) * heat_d[6 + 2 * a, p] - jnp.minimum(v, 0.0) * heat_d[7 + 2 * a, p]
        msg[p, 0:8] = out
        msg[p, 8:16] = fill
        return c

    lax.fori_loop(0, NP, transport, 0, unroll=8)

    for dz, dy, dc in FAR_FIRST:
        p = lax.rem(z + dz, 4) * 8 + lax.rem(y + dy, 4) * 2 + lax.rem(core + dc, 2)
        pltpu.make_async_remote_copy(
            src_ref=msg.at[p], dst_ref=warm_out.at[d],
            send_sem=back_sem.at[0], recv_sem=back_sem.at[1], device_id=(g, p), device_id_type=MESH,
        ).start()
    keep = pltpu.make_async_copy(msg.at[d], warm_out.at[d], load_sem.at[0])
    keep.start()
    fill_copy = pltpu.make_async_copy(fz2.at[pl.ds(1, NP), pl.ds(8, 8)], fill_out, out_sem.at[0])
    fill_copy.start()

    def second(p, c):
        new = collide(f1, p)
        for q in range(19):
            f0[q, p + 1] = new[q]
        return c

    lax.fori_loop(0, NP, second, 0, unroll=2)
    pops_copy = pltpu.make_async_copy(f0.at[:, pl.ds(1, NP)], pops_out, out_sem.at[1])
    pops_copy.start()

    for c in corner0 + z0 + x0 + corner1 + z1 + x1 + end_sends:
        c.wait_send()

    def all_of(ref, count, sem):
        part_of = ref.at[pl.ds(0, count)]
        pltpu.make_async_copy(part_of, part_of, sem).wait()

    all_of(hot_msg, ND - 1, hot_sem.at[0])

    @pl.when(d == 0)
    def _():
        all_of(hot_msg, ND // 2, hot_sem.at[4])

    @pl.when(d == ND - 1)
    def _():
        all_of(hot_msg, ND // 2, hot_sem.at[4])

    keep.wait()
    fill_copy.wait()
    pops_copy.wait()
    all_of(msg, ND - 1, back_sem.at[0])
    all_of(msg, ND - 1, back_sem.at[1])

    @pl.when(d == 0)
    def _():
        all_of(msg, ND // 2, back_sem.at[4])

    @pl.when(d == ND - 1)
    def _():
        all_of(msg, ND // 2, back_sem.at[5])


def finish_kernel(
    pops_mid, fill_mid, warm_mid, ends_mid, energy_in, pops_out, fill_out, energy_out, got, ends, own, done, sem
):
    g, d = lax.axis_index("grp"), lax.axis_index("dev")
    copies = [
        pltpu.make_async_copy(pops_mid, pops_out, sem.at[0]),
        pltpu.make_async_copy(warm_mid, got, sem.at[1]),
        pltpu.make_async_copy(energy_in, own, sem.at[2]),
        pltpu.make_async_copy(ends_mid, ends, sem.at[3]),
        pltpu.make_async_copy(fill_mid, fill_out, sem.at[4]),
    ]
    for c in copies:
        c.start()
    for c in copies[1:4]:
        c.wait()
    lane = lane_iota()
    low = jnp.logical_and(d == 0, g > 0)
    high = jnp.logical_and(d == ND - 1, g < NG - 1)

    def temp(h):
        return jnp.minimum(h, 1.0) + jnp.maximum(h - 1.5, 0.0)

    for e in range(ND):
        cells = slice(e * NL, (e + 1) * NL)
        out = got[e, 0:8] + jnp.where(low, ends[0, e], 0.0) + jnp.where(high, ends[1, e], 0.0)
        warmth = temp(own[0, :, cells])
        for side, other in ((0, e - 1), (1, e + 1)):
            if other < 0 or other >= ND:
                continue
            by, edge = (1, 0) if side == 0 else (NL - 1, NL - 1)
            beyond = temp(own[0, :, other * NL : (other + 1) * NL])
            term = pltpu.roll(got[other, 8:16], by, 1) * (pltpu.roll(beyond, by, 1) - warmth)
            out = out + jnp.where(lane == edge, (0.05 * STEP_TIME) * term, 0.0)
        done[0, :, cells] = out
    last = pltpu.make_async_copy(done, energy_out, sem.at[1])
    last.start()
    last.wait()
    copies[4].wait()
    copies[0].wait()


def shards(populations, fill, flags, specific_energy_grid):
    plane = (NY, NL)
    any_spec = pl.BlockSpec(memory_space=pl.ANY)
    hbm_spec = pl.BlockSpec(memory_space=pltpu.HBM)
    given = [
        pltpu.with_memory_space_constraint(x, pltpu.HBM)
        for x in (populations, fill, flags, specific_energy_grid)
    ]
    pops_mid, fill_mid, warm_mid, ends_mid = pl.pallas_call(
        fluid_kernel,
        out_shape=(
            jax.ShapeDtypeStruct((19, NP) + plane, F32),
            jax.ShapeDtypeStruct((NP,) + plane, F32),
            jax.ShapeDtypeStruct((ND, 16, NL), F32),
            jax.ShapeDtypeStruct((2, ND) + plane, F32),
        ),
        in_specs=[hbm_spec] * 4,
        out_specs=(any_spec,) * 4,
        scratch_shapes=[
            pltpu.VMEM((19, NP + 2) + plane, F32),
            pltpu.VMEM((19, NP + 2) + plane, F32),
            pltpu.VMEM((3, NP + 2, 24, NL), F32),
            pltpu.VMEM((3, NP + 2, 24, NL), F32),
            pltpu.VMEM((NP + 2, 24, NL), F32),
            pltpu.VMEM((10, NP + 2) + plane, F32),
            pltpu.VMEM((10, NP) + plane, F32),
            pltpu.VMEM((19, NP) + plane, F32),
            pltpu.VMEM((4, NP) + plane, F32),
            pltpu.VMEM((5, NP) + plane, F32),
            pltpu.VMEM((NP,) + plane, jnp.int32),
            pltpu.VMEM((4, NP) + plane, F32),
            pltpu.VMEM((NY, (ND + 2) * NL), F32),
            pltpu.VMEM((ND, 16, NL), F32),
            pltpu.VMEM((NP + 2, 16, NL), F32),
            pltpu.VMEM((13, NP) + plane, F32),
            pltpu.VMEM((2, 2, 6) + plane, F32),
            pltpu.VMEM((2, 2, 6) + plane, F32),
            pltpu.VMEM((2, 2, 16, NL), F32),
            pltpu.VMEM((2, 2, 16, NL), F32),
            pltpu.VMEM((2, 2, 2, 16, NL), F32),
            pltpu.VMEM((ND, 16, NL), F32),
            pltpu.VMEM((2,) + plane, F32),
            pltpu.SemaphoreType.DMA((7,)),
            pltpu.SemaphoreType.DMA((2, 8)),
            pltpu.SemaphoreType.DMA((2, 8)),
            pltpu.SemaphoreType.DMA((5,)),
            pltpu.SemaphoreType.DMA((6,)),
            pltpu.SemaphoreType.DMA((2,)),
            pltpu.SemaphoreType.REGULAR,
            pltpu.SemaphoreType.REGULAR,
        ],
        compiler_params=pltpu.CompilerParams(
            collective_id=0, has_side_effects=True, vmem_limit_bytes=40 * 1024 * 1024
        ),
        name="pour",
    )(*given)
    return pl.pallas_call(
        finish_kernel,
        out_shape=(
            jax.ShapeDtypeStruct((19, NP) + plane, F32),
            jax.ShapeDtypeStruct((NP,) + plane, F32),
            jax.ShapeDtypeStruct((1, NY, ND * NL), F32),
        ),
        in_specs=[any_spec] * 5,
        out_specs=(any_spec,) * 3,
        scratch_shapes=[
            pltpu.VMEM((ND, 16, NL), F32),
            pltpu.VMEM((2, ND) + plane, F32),
            pltpu.VMEM((1, NY, ND * NL), F32),
            pltpu.VMEM((1, NY, ND * NL), F32),
            pltpu.SemaphoreType.DMA((5,)),
        ],
        compiler_params=pltpu.CompilerParams(vmem_limit_bytes=8 * 1024 * 1024),
        name="finish",
    )(pops_mid, fill_mid, warm_mid, ends_mid, given[3])


def solution(mesh):
    in_specs = (
        P(None, "grp", None, "dev"),
        P("grp", None, "dev"),
        P("grp", None, "dev"),
        P(("grp", "dev"), None, None),
    )
    out_specs = (P(None, "grp", None, "dev"), P("grp", None, "dev"), P(("grp", "dev"), None, None))
    return jax.shard_map(shards, mesh=mesh, in_specs=in_specs, out_specs=out_specs, check_vma=False)
```

time: 32.4 us -> 29.3 us (0.904)
  Pallas kernels: 31.6 us -> 28.5 us
    pallas_call x1, Pallas kernels: 29.7 us -> 26.5 us  [shards(): pl.pallas_call(fluid_kernel, out_shape=(jax.ShapeDtypeStruct((19, NP) + p...]
where the time goes in v2:
time: 29.3 us; the launch traced here: 29.1 us
  Pallas kernels  28.5 us (97%)
  between operations  0.64 us (2%)
    pallas_call x1, Pallas kernels, shards(): pl.pallas_call(fluid_kernel, out_shape=(jax.ShapeDtypeStruct((19, NP) + p...  26.5 us
    pallas_call x1, Pallas kernels, shards(): pl.pallas_call(finish_kernel, out_shape=(jax.ShapeDtypeStruct((19, NP) +...  2 us

profile of v2, /device:TPU:1, one launch (start us, length us, event | category | flops | bytes accessed | tf_op | source)
XLA Modules:
  0.0 29.1 jit_solution(13092621742740194407)
XLA Ops:
  0.6 26.5 %pour.1 = (f32[19,32,8,128]{3,2,1,0:T(8,128)S(1)}, f32[32,8,128]{2,1,0:T(8,128)S(1)}, f32[32,16,128]{2,1,0:T(8,128)S(1)}, f32[2,32,8,128]{3,2,1,0:T(8,128)S(1)}) custom-call(f32[19,32,8,128]{3,2,1,0:T(8,128)} %pops_in.1, f32[32,8,128]{2,1,0:T(8,128)} %fill_in.1, s32[32,8,128]{2,1,0:T(8,128)} %flags_in.1, f32[1,8,4096]{2,1,0:T(8,128)} %energy_in.3), custom_call_target="tpu_custom_call" | custom-call | tf_op jit(solution)/shard_map/pour/pallas_call | solution.py:662
  27.1 2.0 %finish.1 = (f32[19,32,8,128]{3,2,1,0:T(8,128)}, f32[32,8,128]{2,1,0:T(8,128)}, f32[1,8,4096]{2,1,0:T(8,128)}) custom-call(f32[19,32,8,128]{3,2,1,0:T(8,128)S(1)} %get-tuple-element.7.pops_mid, f32[32,8,128]{2,1,0:T(8,128)S(1)} %get-tuple-element.8.fill_mid, f32[32,16,128]{2,1,0:T(8,128)S(1)} %get-tuple-element.9.warm_mid, ...), custom_call_target="tpu_custom_call" | custom-call | tf_op jit(solution)/shard_map/finish/pallas_call | solution.py:710

commit v3 on v2

--- a/solution.py
+++ b/solution.py
@@ -38,17 +38,11 @@
 NG, ND, NP, NY, NL = 4, 32, 32, 8, 128
 FLAT = (1, 2, 3, 4, 7, 8, 9, 10)
 UP = (5, 15, 18, 11, 14)
-DOWN = (6, 16, 17, 13, 12)
+DOWN = (6, 17, 16, 13, 12)
 CROSS = UP + DOWN
 EAST = (1, 7, 9, 11, 13)
 WEST = (2, 8, 10, 12, 14)
 Z_PAIRS = (5, 11, 13, 15, 17)
-
-
-FAR_FIRST = sorted(
-    ((dz, dy, dc) for dz in range(4) for dy in range(4) for dc in range(2) if dz or dy or dc),
-    key=lambda at: -(min(at[0], 4 - at[0]) + min(at[1], 4 - at[1])),
-)
 
 
 def opposite(q):
@@ -83,29 +77,24 @@
     return out, sum(s.values())
 
 
-def pack_columns(tops, bottoms, fill, p, acc, lane):
-    spot = lane & 31
-    here = spot == p
-    east = lane == ((p + 1) & 31)
-    west = lane == 32 + ((p + 31) & 31)
+def pack_columns(ups, downs, fill, p, acc, lane):
+    here = (lane >> 1) == p
+    there = (lane >> 1) == p + 32
+
+    def both(k):
+        return jnp.where(lane == NL - 1, ups[k], downs[k])
+
     out = []
-    for side, (cols, edge) in enumerate(((tops, NL - 1), (bottoms, 0))):
-        a, b = acc[2 * side], acc[2 * side + 1]
-        v = spread(cols[0], edge)
-        v = jnp.where(lane >= 32, spread(cols[1], edge), v)
-        v = jnp.where(lane >= 64, spread(cols[2], edge), v)
-        v = jnp.where(lane >= 96, spread(fill, edge), v)
-        a = jnp.where(here, v, a)
-        b = jnp.where(east, spread(cols[3], edge), b)
-        b = jnp.where(west, spread(cols[4], edge), b)
-        out += [a, b]
+    for a, first, second in ((acc[0], both(0), both(1)), (acc[1], both(2), fill), (acc[2], both(3), both(4))):
+        a = jnp.where(here, pltpu.roll(first, 2 * p + 1, 1), a)
+        out.append(jnp.where(there, pltpu.roll(second, 2 * p + 65, 1), a))
     return tuple(out)
 
 
 def fluid_kernel(
     pops_in, fill_in, flags_in, energy_in,
     pops_out, fill_out, warm_out, ends_out,
-    f0, f1, fz0, fz1, fz2, roll_z, halo_s, g_s, part, eqs, flags, vel, own_e, hot_msg, hbuf, heat_d,
+    f0, f1, fz0, fz1, fz2, roll_z, halo_s, columns, g_s, part, eqs, flags, vel, own_e, hot_msg, hbuf, heat_d,
     xs, xr, zs, zr, zd, msg, end_msg,
     load_sem, send_sem, recv_sem, hot_sem, back_sem, out_sem, group_sem, next_sem,
 ):
@@ -116,19 +105,6 @@
     row = lax.broadcasted_iota(jnp.int32, (NY, NL), 0)
     zero8 = jnp.zeros((NY, NL), F32)
 
-    def load(src, dst, n):
-        c = pltpu.make_async_copy(src, dst, load_sem.at[n])
-        c.start()
-        return c
-
-    def load_pops(q, count, n):
-        return load(pops_in.at[pl.ds(q, count)], f0.at[pl.ds(q, count), pl.ds(1, NP)], n)
-
-    fill_load = load(fill_in, fz0.at[1, pl.ds(1, NP), pl.ds(8, 8)], 0)
-    cross_loads = [load_pops(11, 8, 1), load_pops(5, 2, 2)]
-    more_loads = [load_pops(0, 5, 3), load_pops(7, 4, 4), load(flags_in, flags, 5)]
-    energy_load = load(energy_in.at[0], own_e.at[:, pl.ds(NL, ND * NL)], 6)
-
     z, y, core = lax.div(d, 8), lax.rem(lax.div(d, 2), 4), lax.rem(d, 2)
     barrier = pltpu.get_barrier_semaphore()
     column_peers = [(g, lax.rem(d + 8 * k, ND)) for k in range(1, 4)]
@@ -138,6 +114,19 @@
     for to in near:
         pl.semaphore_signal(barrier, inc=1, device_id=to, device_id_type=MESH)
 
+    def load(src, dst, n):
+        c = pltpu.make_async_copy(src, dst, load_sem.at[n])
+        c.start()
+        return c
+
+    def load_pops(q, count, n):
+        return load(pops_in.at[pl.ds(q, count)], f0.at[pl.ds(q, count), pl.ds(1, NP)], n)
+
+    fill_load = load(fill_in, fz0.at[1, pl.ds(1, NP), pl.ds(8, 8)], 0)
+    cross_loads = [load_pops(11, 8, 1), load_pops(5, 2, 2)]
+    more_loads = [load_pops(0, 5, 3), load_pops(7, 4, 4), load(flags_in, flags, 5)]
+    energy_load = load(energy_in.at[0], own_e.at[:, pl.ds(NL, ND * NL)], 6)
+
     def clear(p, c):
         for k in range(3):
             for ref in (fz0, fz1):
@@ -167,13 +156,13 @@
 
     def z_sends(t):
         return [
-            send(t, zs.at[t, side], zr.at[t, side], 2 + side, (g, to))
+            send(t, zs.at[t], zr.at[t, side], 2 + side, (g, to))
             for side, to in ((0, up), (1, down))
         ]
 
     def corner_sends(t):
         return [
-            send(t, zs.at[t, side], zd.at[t, side, k], 4 + 2 * side + k, (gg, to))
+            send(t, zs.at[t], zd.at[t, side, k], 4 + 2 * side + k, (gg, to))
             for side, to in ((0, up), (1, down))
             for k, gg in ((0, east), (1, west))
         ]
@@ -187,9 +176,8 @@
         xs[t, 1, 5] = fz[1, 1, 8:16]
 
     def store_z(t, acc):
-        for side in range(2):
-            zs[t, side, 0:8] = acc[2 * side]
-            zs[t, side, 8:16] = acc[2 * side + 1]
+        for k in range(3):
+            zs[t, 8 * k : 8 * k + 8] = acc[k]
 
     def started(copies):
         for c in copies:
@@ -209,7 +197,7 @@
             [f0[q, p + 1] for q in UP], [f0[q, p + 1] for q in DOWN], fz0[1, p + 1, 8:16], p, acc, lane
         )
 
-    acc0 = (zero8,) * 4
+    acc0 = (zero8,) * 3
     store_z(0, lax.fori_loop(0, NP, pack0, acc0, unroll=8))
 
     pl.semaphore_wait(barrier, len(near))
@@ -312,7 +300,7 @@
             for q in dirs:
                 cx, cy, cz = VELOCITIES[q]
                 k = CROSS.index(q)
-                incoming = jnp.where(lane == edge, halo_s[k, p], roll_z[k, p + 1 - cx])
+                incoming = jnp.where(lane == edge, halo_s[k % 5, p], roll_z[k, p + 1 - cx])
                 incoming = shift_rows(incoming, cy)
                 beside = fz[1 - cz, p + 1 - cx, 8 - cy : 16 - cy]
                 empty = beside == 0.0
@@ -337,20 +325,29 @@
         )
 
     def cross(t, f, fz, fill_ref, corner):
-        inside = (d > 0, d < ND - 1)
-        fills = [jnp.where(inside[side], zr[t, side, 0:8], 0.0) for side in range(2)]
+        odd = (lane & 1) == 1
+        inside = jnp.logical_or(jnp.logical_and(odd, d > 0), jnp.logical_and(jnp.logical_not(odd), d < ND - 1))
+
+        def turned(low, high, k):
+            rows = slice(8 * (k // 2), 8 * (k // 2) + 8)
+            by = 64 * (k % 2)
+            return jnp.where(odd, pltpu.roll(low[rows], by + 1, 1), pltpu.roll(high[rows], (by + NL - 1) % NL, 1))
+
+        main = (zr.at[t, 0], zr.at[t, 1])
+        for k, half in enumerate((0, 1, 2, 4, 5)):
+            columns[k] = turned(*main, half)
+        columns[5] = jnp.where(inside, turned(*main, 3), 0.0)
+
+        def to_edges(k, p):
+            return pltpu.roll(columns[k], lax.rem(2 * NL - 1 - 2 * p, NL), 1)
 
         def halos(p):
-            for side, dirs in enumerate((UP, DOWN)):
-                edge = 0 if side == 0 else NL - 1
-                for k, q in enumerate(dirs):
-                    spot = 32 * k if k < 3 else 32 * (k - 3)
-                    rows = zr[t, side, 0:8] if k < 3 else zr[t, side, 8:16]
-                    halo_s[CROSS.index(q), p] = pltpu.roll(rows, lax.rem(NL + edge - spot - p, NL), 1)
+            for k in range(5):
+                halo_s[k, p] = to_edges(k, p - VELOCITIES[UP[k]][0])
 
         def fill_columns(p):
-            for side, edge, k in ((0, 0, 0), (1, NL - 1, 2)):
-                new = pltpu.roll(fills[side], lax.rem(2 * NL + edge - 96 - p, NL), 1)
+            new = to_edges(5, p)
+            for edge, k in ((0, 0), (NL - 1, 2)):
                 fz[k, p + 1, 8:16] = jnp.where(lane == edge, new, fz[k, p + 1, 8:16])
 
         def prepare(base):
@@ -375,16 +372,21 @@
         lax.fori_loop(0, NP // 8 - 1, mid, 0)
 
         arrived(corner)
-        for side in range(2):
-            b = jnp.where(lane == 0, zd[t, side, 0, 8:16], zr[t, side, 8:16])
-            b = jnp.where(lane == 63, zd[t, side, 1, 8:16], b)
-            zr[t, side, 8:16] = b
-            edge, k, by = ((0, 0, 1), (NL - 1, 2, NL - 1))[side]
-            for at, src, spot, ok in ((0, 0, 127, g > 0), (NP + 1, 1, 96, g < NG - 1)):
-                old = pltpu.roll(fz[1, at, 8:16], by, 1)
-                new = spread(zd[t, side, src, 0:8], spot)
-                ok = jnp.logical_and(ok, inside[side])
-                fz[k, at, 8:16] = jnp.where(lane == edge, jnp.where(ok, new, 0.0), old)
+        west_lanes, east_lanes = lane >= NL - 2, (lane >> 1) == 32
+        last_of = (zd.at[t, 0, 0], zd.at[t, 1, 0])
+        first_of = (zd.at[t, 0, 1], zd.at[t, 1, 1])
+        columns[3] = jnp.where(west_lanes, pltpu.roll(turned(*last_of, 4), 64, 1), columns[3])
+        columns[4] = jnp.where(east_lanes, pltpu.roll(turned(*first_of, 5), 64, 1), columns[4])
+        fills = columns[5]
+        ghost = jnp.where(jnp.logical_and(inside, g > 0), pltpu.roll(turned(*last_of, 3), 64, 1), 0.0)
+        fills = jnp.where(west_lanes, ghost, fills)
+        ghost = jnp.where(jnp.logical_and(inside, g < NG - 1), pltpu.roll(turned(*first_of, 3), 64, 1), 0.0)
+        columns[5] = jnp.where(east_lanes, ghost, fills)
+        for at in (0, NP + 1):
+            fz[0, at, 8:16] = pltpu.roll(fz[1, at, 8:16], 1, 1)
+            fz[2, at, 8:16] = pltpu.roll(fz[1, at, 8:16], NL - 1, 1)
+        fill_columns(-1)
+        fill_columns(NP)
         for j in range(4):
             halos(j)
             halos(NP - 4 + j)
@@ -555,14 +557,17 @@
         msg[p, 8:16] = fill
         return c
 
-    lax.fori_loop(0, NP, transport, 0, unroll=8)
-
-    for dz, dy, dc in FAR_FIRST:
-        p = lax.rem(z + dz, 4) * 8 + lax.rem(y + dy, 4) * 2 + lax.rem(core + dc, 2)
-        pltpu.make_async_remote_copy(
-            src_ref=msg.at[p], dst_ref=warm_out.at[d],
-            send_sem=back_sem.at[0], recv_sem=back_sem.at[1], device_id=(g, p), device_id_type=MESH,
-        ).start()
+    for dz in (2, 1, 3, 0):
+        z_to = lax.rem(z + dz, 4)
+        for j in range(8):
+            transport(8 * z_to + j, 0)
+        for dy, dc in ((2, 0), (2, 1), (1, 0), (1, 1), (3, 0), (3, 1), (0, 1), (0, 0)):
+            if dz or dy or dc:
+                p = 8 * z_to + lax.rem(y + dy, 4) * 2 + lax.rem(core + dc, 2)
+                pltpu.make_async_remote_copy(
+                    src_ref=msg.at[p], dst_ref=warm_out.at[d],
+                    send_sem=back_sem.at[0], recv_sem=back_sem.at[1], device_id=(g, p), device_id_type=MESH,
+                ).start()
     keep = pltpu.make_async_copy(msg.at[d], warm_out.at[d], load_sem.at[0])
     keep.start()
     fill_copy = pltpu.make_async_copy(fz2.at[pl.ds(1, NP), pl.ds(8, 8)], fill_out, out_sem.at[0])
@@ -574,9 +579,15 @@
             f0[q, p + 1] = new[q]
         return c
 
-    lax.fori_loop(0, NP, second, 0, unroll=2)
-    pops_copy = pltpu.make_async_copy(f0.at[:, pl.ds(1, NP)], pops_out, out_sem.at[1])
-    pops_copy.start()
+    pops_copies = []
+    for base in range(0, NP, 8):
+        lax.fori_loop(base, base + 8, second, 0, unroll=4)
+        pops_copies.append(
+            pltpu.make_async_copy(
+                f0.at[:, pl.ds(1 + base, 8)], pops_out.at[:, pl.ds(base, 8)], out_sem.at[1 + base // 8]
+            )
+        )
+        pops_copies[-1].start()
 
     for c in corner0 + z0 + x0 + corner1 + z1 + x1 + end_sends:
         c.wait_send()
@@ -597,7 +608,8 @@
 
     keep.wait()
     fill_copy.wait()
-    pops_copy.wait()
+    for c in pops_copies:
+        c.wait()
     all_of(msg, ND - 1, back_sem.at[0])
     all_of(msg, ND - 1, back_sem.at[1])
 
@@ -632,6 +644,7 @@
     def temp(h):
         return jnp.minimum(h, 1.0) + jnp.maximum(h - 1.5, 0.0)
 
+    halves = []
     for e in range(ND):
         cells = slice(e * NL, (e + 1) * NL)
         out = got[e, 0:8] + jnp.where(low, ends[0, e], 0.0) + jnp.where(high, ends[1, e], 0.0)
@@ -644,9 +657,14 @@
             term = pltpu.roll(got[other, 8:16], by, 1) * (pltpu.roll(beyond, by, 1) - warmth)
             out = out + jnp.where(lane == edge, (0.05 * STEP_TIME) * term, 0.0)
         done[0, :, cells] = out
-    last = pltpu.make_async_copy(done, energy_out, sem.at[1])
-    last.start()
-    last.wait()
+        if e % (ND // 2) == ND // 2 - 1:
+            half = pl.ds((e // (ND // 2)) * (ND // 2) * NL, ND // 2 * NL)
+            halves.append(
+                pltpu.make_async_copy(done.at[:, :, half], energy_out.at[:, :, half], sem.at[1 + len(halves)])
+            )
+            halves[-1].start()
+    for c in halves:
+        c.wait()
     copies[4].wait()
     copies[0].wait()
 
@@ -676,7 +694,8 @@
             pltpu.VMEM((3, NP + 2, 24, NL), F32),
             pltpu.VMEM((NP + 2, 24, NL), F32),
             pltpu.VMEM((10, NP + 2) + plane, F32),
-            pltpu.VMEM((10, NP) + plane, F32),
+            pltpu.VMEM((5, NP) + plane, F32),
+            pltpu.VMEM((6,) + plane, F32),
             pltpu.VMEM((19, NP) + plane, F32),
             pltpu.VMEM((4, NP) + plane, F32),
             pltpu.VMEM((5, NP) + plane, F32),
@@ -688,9 +707,9 @@
             pltpu.VMEM((13, NP) + plane, F32),
             pltpu.VMEM((2, 2, 6) + plane, F32),
             pltpu.VMEM((2, 2, 6) + plane, F32),
-            pltpu.VMEM((2, 2, 16, NL), F32),
-            pltpu.VMEM((2, 2, 16, NL), F32),
-            pltpu.VMEM((2, 2, 2, 16, NL), F32),
+            pltpu.VMEM((2, 24, NL), F32),
+            pltpu.VMEM((2, 2, 24, NL), F32),
+            pltpu.VMEM((2, 2, 2, 24, NL), F32),
             pltpu.VMEM((ND, 16, NL), F32),
             pltpu.VMEM((2,) + plane, F32),
             pltpu.SemaphoreType.DMA((7,)),
@@ -698,7 +717,7 @@
             pltpu.SemaphoreType.DMA((2, 8)),
             pltpu.SemaphoreType.DMA((5,)),
             pltpu.SemaphoreType.DMA((6,)),
-            pltpu.SemaphoreType.DMA((2,)),
+            pltpu.SemaphoreType.DMA((5,)),
             pltpu.SemaphoreType.REGULAR,
             pltpu.SemaphoreType.REGULAR,
         ],

time: 29.3 us -> 28.9 us (0.986)
  Pallas kernels: 28.5 us -> 28.1 us
    pallas_call x1, Pallas kernels: 26.5 us -> 26.1 us  [shards(): pl.pallas_call(fluid_kernel, out_shape=(jax.ShapeDtypeStruct((19, NP) + p...]
where the time goes in v3:
time: 28.9 us; the launch traced here: 28.7 us
  Pallas kernels  28.1 us (97%)
  between operations  0.64 us (2%)
    pallas_call x1, Pallas kernels, shards(): pl.pallas_call(fluid_kernel, out_shape=(jax.ShapeDtypeStruct((19, NP) + p...  26.1 us
    pallas_call x1, Pallas kernels, shards(): pl.pallas_call(finish_kernel, out_shape=(jax.ShapeDtypeStruct((19, NP) +...  1.97 us

profile of v3, /device:TPU:1, one launch (start us, length us, event | category | flops | bytes accessed | tf_op | source)
XLA Modules:
  0.0 28.7 jit_solution(14975253837534797759)
XLA Ops:
  0.6 26.1 %pour.1 = (f32[19,32,8,128]{3,2,1,0:T(8,128)S(1)}, f32[32,8,128]{2,1,0:T(8,128)S(1)}, f32[32,16,128]{2,1,0:T(8,128)S(1)}, f32[2,32,8,128]{3,2,1,0:T(8,128)S(1)}) custom-call(f32[19,32,8,128]{3,2,1,0:T(8,128)} %pops_in.1, f32[32,8,128]{2,1,0:T(8,128)} %fill_in.1, s32[32,8,128]{2,1,0:T(8,128)} %flags_in.1, f32[1,8,4096]{2,1,0:T(8,128)} %energy_in.3), custom_call_target="tpu_custom_call" | custom-call | tf_op jit(solution)/shard_map/pour/pallas_call | solution.py:680
  26.7 2.0 %finish.1 = (f32[19,32,8,128]{3,2,1,0:T(8,128)}, f32[32,8,128]{2,1,0:T(8,128)}, f32[1,8,4096]{2,1,0:T(8,128)}) custom-call(f32[19,32,8,128]{3,2,1,0:T(8,128)S(1)} %get-tuple-element.7.pops_mid, f32[32,8,128]{2,1,0:T(8,128)S(1)} %get-tuple-element.8.fill_mid, f32[32,16,128]{2,1,0:T(8,128)S(1)} %get-tuple-element.9.warm_mid, ...), custom_call_target="tpu_custom_call" | custom-call | tf_op jit(solution)/shard_map/finish/pallas_call | solution.py:729

commit v4 on v3

--- a/solution.py
+++ b/solution.py
@@ -45,6 +45,12 @@
 Z_PAIRS = (5, 11, 13, 15, 17)
 
 
+FAR_FIRST = sorted(
+    ((dz, dy) for dz in range(4) for dy in range(4)),
+    key=lambda at: -(min(at[0], 4 - at[0]) + min(at[1], 4 - at[1])),
+)
+
+
 def opposite(q):
     return q + 1 if q % 2 == 1 else q - 1
 
@@ -96,7 +102,7 @@
     pops_out, fill_out, warm_out, ends_out,
     f0, f1, fz0, fz1, fz2, roll_z, halo_s, columns, g_s, part, eqs, flags, vel, own_e, hot_msg, hbuf, heat_d,
     xs, xr, zs, zr, zd, msg, end_msg,
-    load_sem, send_sem, recv_sem, hot_sem, back_sem, out_sem, group_sem, next_sem,
+    load_sem, send_sem, recv_sem, hot_sem, back_sem, out_sem, next_sem,
 ):
     g, d = lax.axis_index("grp"), lax.axis_index("dev")
     up, down = lax.rem(d + 1, ND), lax.rem(d + ND - 1, ND)
@@ -107,10 +113,14 @@
 
     z, y, core = lax.div(d, 8), lax.rem(lax.div(d, 2), 4), lax.rem(d, 2)
     barrier = pltpu.get_barrier_semaphore()
-    column_peers = [(g, lax.rem(d + 8 * k, ND)) for k in range(1, 4)]
     x_peers = [(east, d), (west, d)]
-    near = [(gg, dd) for dd in (up, down, d) for gg in (east, west)] + [(g, up), (g, down)]
-    near += column_peers + [(g, 8 * z + lax.rem(d + k, 8)) for k in range(1, 8)]
+    near = [(gg, dd) for dd in (up, down) for gg in (east, west)]
+    for dz, dy in FAR_FIRST:
+        for dc in range(2):
+            if dz or dy or dc:
+                to = lax.rem(z + dz, 4) * 8 + lax.rem(y + dy, 4) * 2 + lax.rem(core + dc, 2)
+                near.append((g, to))
+    near += x_peers
     for to in near:
         pl.semaphore_signal(barrier, inc=1, device_id=to, device_id_type=MESH)
 
@@ -200,9 +210,22 @@
     acc0 = (zero8,) * 3
     store_z(0, lax.fori_loop(0, NP, pack0, acc0, unroll=8))
 
+    energy_load.wait()
+
+    def block_of(e):
+        return own_e[:, pl.ds(pl.multiple_of((e + 1) * NL, NL), NL)]
+
+    def hot_build(e, c):
+        hot_msg[e, 0:8] = block_of(e)
+        beside = jnp.where(lane == 0, pltpu.roll(block_of(e - 1), 1, 1), pltpu.roll(block_of(e + 1), NL - 1, 1))
+        hot_msg[e, 8:16] = beside
+        return c
+
+    lax.fori_loop(0, ND, hot_build, 0, unroll=8)
+
     pl.semaphore_wait(barrier, len(near))
-    for to in column_peers:
-        pl.semaphore_signal(group_sem, inc=1, device_id=to, device_id_type=MESH)
+    for to in x_peers:
+        pl.semaphore_signal(next_sem, inc=1, device_id=to, device_id_type=MESH)
 
     corner0 = started(corner_sends(0))
     z0 = started(z_sends(0))
@@ -210,6 +233,19 @@
         c.wait()
     fill_x(0, f0, fz0)
     x0 = started(x_sends(0))
+
+    def hot_start(i, c):
+        to = lax.rem(d + i, ND)
+        pltpu.make_async_remote_copy(
+            src_ref=hot_msg.at[to], dst_ref=hbuf.at[d + 1],
+            send_sem=hot_sem.at[0], recv_sem=hot_sem.at[1], device_id=(g, to), device_id_type=MESH,
+        ).start()
+        return c
+
+    lax.fori_loop(1, ND, hot_start, 0)
+    own = pltpu.make_async_copy(hot_msg.at[d], hbuf.at[d + 1], load_sem.at[0])
+    own.start()
+
 
     def local_part(f, fz):
         def body(p):
@@ -420,35 +456,6 @@
         return new
 
     local_inner(f0, fz0)
-
-    energy_load.wait()
-
-    def block_of(e):
-        return own_e[:, pl.ds(pl.multiple_of((e + 1) * NL, NL), NL)]
-
-    def hot_build(e, c):
-        hot_msg[e, 0:8] = block_of(e)
-        beside = jnp.where(lane == 0, pltpu.roll(block_of(e - 1), 1, 1), pltpu.roll(block_of(e + 1), NL - 1, 1))
-        hot_msg[e, 8:16] = beside
-        return c
-
-    lax.fori_loop(0, ND, hot_build, 0, unroll=8)
-
-    pl.semaphore_wait(group_sem, len(column_peers))
-    for to in x_peers:
-        pl.semaphore_signal(next_sem, inc=1, device_id=to, device_id_type=MESH)
-
-    def hot_start(i, c):
-        to = lax.rem(d + i, ND)
-        pltpu.make_async_remote_copy(
-            src_ref=hot_msg.at[to], dst_ref=hbuf.at[d + 1],
-            send_sem=hot_sem.at[0], recv_sem=hot_sem.at[1], device_id=(g, to), device_id_type=MESH,
-        ).start()
-        return c
-
-    lax.fori_loop(1, ND, hot_start, 0)
-    own = pltpu.make_async_copy(hot_msg.at[d], hbuf.at[d + 1], load_sem.at[0])
-    own.start()
 
     pl.semaphore_wait(next_sem, len(x_peers))
 
@@ -719,7 +726,6 @@
             pltpu.SemaphoreType.DMA((6,)),
             pltpu.SemaphoreType.DMA((5,)),
             pltpu.SemaphoreType.REGULAR,
-            pltpu.SemaphoreType.REGULAR,
         ],
         compiler_params=pltpu.CompilerParams(
             collective_id=0, has_side_effects=True, vmem_limit_bytes=40 * 1024 * 1024

time: 28.9 us -> 28.8 us (level)
  no operation moved by 1% of the time
where the time goes in v4:
time: 28.8 us; the launch traced here: 28.6 us
  Pallas kernels  28 us (97%)
  between operations  0.64 us (2%)
    pallas_call x1, Pallas kernels, shards(): pl.pallas_call(fluid_kernel, out_shape=(jax.ShapeDtypeStruct((19, NP) + p...  26 us
    pallas_call x1, Pallas kernels, shards(): pl.pallas_call(finish_kernel, out_shape=(jax.ShapeDtypeStruct((19, NP) +...  1.97 us

profile of v4, /device:TPU:1, one launch (start us, length us, event | category | flops | bytes accessed | tf_op | source)
XLA Modules:
  0.0 28.6 jit_solution(1377659669993380464)
XLA Ops:
  0.6 26.0 %pour.1 = (f32[19,32,8,128]{3,2,1,0:T(8,128)S(1)}, f32[32,8,128]{2,1,0:T(8,128)S(1)}, f32[32,16,128]{2,1,0:T(8,128)S(1)}, f32[2,32,8,128]{3,2,1,0:T(8,128)S(1)}) custom-call(f32[19,32,8,128]{3,2,1,0:T(8,128)} %pops_in.1, f32[32,8,128]{2,1,0:T(8,128)} %fill_in.1, s32[32,8,128]{2,1,0:T(8,128)} %flags_in.1, f32[1,8,4096]{2,1,0:T(8,128)} %energy_in.3), custom_call_target="tpu_custom_call" | custom-call | tf_op jit(solution)/shard_map/pour/pallas_call | solution.py:687
  26.6 2.0 %finish.1 = (f32[19,32,8,128]{3,2,1,0:T(8,128)}, f32[32,8,128]{2,1,0:T(8,128)}, f32[1,8,4096]{2,1,0:T(8,128)}) custom-call(f32[19,32,8,128]{3,2,1,0:T(8,128)S(1)} %get-tuple-element.7.pops_mid, f32[32,8,128]{2,1,0:T(8,128)S(1)} %get-tuple-element.8.fill_mid, f32[32,16,128]{2,1,0:T(8,128)S(1)} %get-tuple-element.9.warm_mid, ...), custom_call_target="tpu_custom_call" | custom-call | tf_op jit(solution)/shard_map/finish/pallas_call | solution.py:735

commit v5 on v4

--- a/solution.py
+++ b/solution.py
@@ -101,7 +101,7 @@
     pops_in, fill_in, flags_in, energy_in,
     pops_out, fill_out, warm_out, ends_out,
     f0, f1, fz0, fz1, fz2, roll_z, halo_s, columns, g_s, part, eqs, flags, vel, own_e, hot_msg, hbuf, heat_d,
-    xs, xr, zs, zr, zd, msg, end_msg,
+    xs, xr, zs, zr, zd, msg, turned, end_msg,
     load_sem, send_sem, recv_sem, hot_sem, back_sem, out_sem, next_sem,
 ):
     g, d = lax.axis_index("grp"), lax.axis_index("dev")
@@ -547,6 +547,12 @@
     for c in end_sends:
         c.start()
 
+    def edge_fill(p, acc):
+        return jnp.where((lane >> 1) == p, pltpu.roll(fz2[p + 1, 8:16], 2 * p + 1, 1), acc)
+
+    edges = lax.fori_loop(0, NP, edge_fill, zero8, unroll=16)
+    turned[...] = jnp.concatenate([edges] * (NL // NY), axis=0).T
+
     def transport(p, c):
         fill = fz2[p + 1, 8:16]
         beside = (
@@ -561,7 +567,7 @@
             v = vel[1 + a, p]
             out = out + jnp.maximum(v, 0.0) * heat_d[6 + 2 * a, p] - jnp.minimum(v, 0.0) * heat_d[7 + 2 * a, p]
         msg[p, 0:8] = out
-        msg[p, 8:16] = fill
+        msg[p, 8:10] = turned[pl.ds(2 * p, 2)]
         return c
 
     for dz in (2, 1, 3, 0):
@@ -572,10 +578,10 @@
             if dz or dy or dc:
                 p = 8 * z_to + lax.rem(y + dy, 4) * 2 + lax.rem(core + dc, 2)
                 pltpu.make_async_remote_copy(
-                    src_ref=msg.at[p], dst_ref=warm_out.at[d],
+                    src_ref=msg.at[p, pl.ds(0, 10)], dst_ref=warm_out.at[d, pl.ds(0, 10)],
                     send_sem=back_sem.at[0], recv_sem=back_sem.at[1], device_id=(g, p), device_id_type=MESH,
                 ).start()
-    keep = pltpu.make_async_copy(msg.at[d], warm_out.at[d], load_sem.at[0])
+    keep = pltpu.make_async_copy(msg.at[d, pl.ds(0, 10)], warm_out.at[d, pl.ds(0, 10)], load_sem.at[0])
     keep.start()
     fill_copy = pltpu.make_async_copy(fz2.at[pl.ds(1, NP), pl.ds(8, 8)], fill_out, out_sem.at[0])
     fill_copy.start()
@@ -617,8 +623,9 @@
     fill_copy.wait()
     for c in pops_copies:
         c.wait()
-    all_of(msg, ND - 1, back_sem.at[0])
-    all_of(msg, ND - 1, back_sem.at[1])
+    sent = msg.at[pl.ds(0, ND - 1), pl.ds(0, 10)]
+    for n in range(2):
+        pltpu.make_async_copy(sent, sent, back_sem.at[n]).wait()
 
     @pl.when(d == 0)
     def _():
@@ -630,7 +637,7 @@
 
 
 def finish_kernel(
-    pops_mid, fill_mid, warm_mid, ends_mid, energy_in, pops_out, fill_out, energy_out, got, ends, own, done, sem
+    pops_mid, fill_mid, warm_mid, ends_mid, energy_in, pops_out, fill_out, energy_out, got, ends, own, done, rows, sem
 ):
     g, d = lax.axis_index("grp"), lax.axis_index("dev")
     copies = [
@@ -651,6 +658,10 @@
     def temp(h):
         return jnp.minimum(h, 1.0) + jnp.maximum(h - 1.5, 0.0)
 
+    rows[...] = jnp.zeros((NL, NL), F32)
+    for e in range(ND):
+        rows[2 * e : 2 * e + 2] = got[e, 8:10]
+    edges = rows[...].T[0:NY]
     halves = []
     for e in range(ND):
         cells = slice(e * NL, (e + 1) * NL)
@@ -661,7 +672,8 @@
                 continue
             by, edge = (1, 0) if side == 0 else (NL - 1, NL - 1)
             beyond = temp(own[0, :, other * NL : (other + 1) * NL])
-            term = pltpu.roll(got[other, 8:16], by, 1) * (pltpu.roll(beyond, by, 1) - warmth)
+            at = 2 * other + side
+            term = pltpu.roll(edges, (edge - at) % NL, 1) * (pltpu.roll(beyond, by, 1) - warmth)
             out = out + jnp.where(lane == edge, (0.05 * STEP_TIME) * term, 0.0)
         done[0, :, cells] = out
         if e % (ND // 2) == ND // 2 - 1:
@@ -718,6 +730,7 @@
             pltpu.VMEM((2, 2, 24, NL), F32),
             pltpu.VMEM((2, 2, 2, 24, NL), F32),
             pltpu.VMEM((ND, 16, NL), F32),
+            pltpu.VMEM((NL, NL), F32),
             pltpu.VMEM((2,) + plane, F32),
             pltpu.SemaphoreType.DMA((7,)),
             pltpu.SemaphoreType.DMA((2, 8)),
@@ -746,6 +759,7 @@
             pltpu.VMEM((2, ND) + plane, F32),
             pltpu.VMEM((1, NY, ND * NL), F32),
             pltpu.VMEM((1, NY, ND * NL), F32),
+            pltpu.VMEM((NL, NL), F32),
             pltpu.SemaphoreType.DMA((5,)),
         ],
         compiler_params=pltpu.CompilerParams(vmem_limit_bytes=8 * 1024 * 1024),

time: 28.8 us -> 28.3 us (0.983)
  Pallas kernels: 28 us -> 27.5 us
    pallas_call x1, Pallas kernels: 26 us -> 25.5 us  [shards(): pl.pallas_call(fluid_kernel, out_shape=(jax.ShapeDtypeStruct((19, NP) + p...]
where the time goes in v5:
time: 28.3 us; the launch traced here: 28.1 us
  Pallas kernels  27.5 us (97%)
  between operations  0.64 us (2%)
    pallas_call x1, Pallas kernels, shards(): pl.pallas_call(fluid_kernel, out_shape=(jax.ShapeDtypeStruct((19, NP) + p...  25.5 us
    pallas_call x1, Pallas kernels, shards(): pl.pallas_call(finish_kernel, out_shape=(jax.ShapeDtypeStruct((19, NP) +...  2.01 us

profile of v5, /device:TPU:1, one launch (start us, length us, event | category | flops | bytes accessed | tf_op | source)
XLA Modules:
  0.0 28.1 jit_solution(9965420551857250058)
XLA Ops:
  0.6 25.5 %pour.1 = (f32[19,32,8,128]{3,2,1,0:T(8,128)S(1)}, f32[32,8,128]{2,1,0:T(8,128)S(1)}, f32[32,16,128]{2,1,0:T(8,128)S(1)}, f32[2,32,8,128]{3,2,1,0:T(8,128)S(1)}) custom-call(f32[19,32,8,128]{3,2,1,0:T(8,128)} %pops_in.1, f32[32,8,128]{2,1,0:T(8,128)} %fill_in.1, s32[32,8,128]{2,1,0:T(8,128)} %flags_in.1, f32[1,8,4096]{2,1,0:T(8,128)} %energy_in.3), custom_call_target="tpu_custom_call" | custom-call | tf_op jit(solution)/shard_map/pour/pallas_call | solution.py:699
  26.1 2.0 %finish.1 = (f32[19,32,8,128]{3,2,1,0:T(8,128)}, f32[32,8,128]{2,1,0:T(8,128)}, f32[1,8,4096]{2,1,0:T(8,128)}) custom-call(f32[19,32,8,128]{3,2,1,0:T(8,128)S(1)} %get-tuple-element.7.pops_mid, f32[32,8,128]{2,1,0:T(8,128)S(1)} %get-tuple-element.8.fill_mid, f32[32,16,128]{2,1,0:T(8,128)S(1)} %get-tuple-element.9.warm_mid, ...), custom_call_target="tpu_custom_call" | custom-call | tf_op jit(solution)/shard_map/finish/pallas_call | solution.py:748

commit v6 on v5

--- a/solution.py
+++ b/solution.py
@@ -435,15 +435,15 @@
 
         lax.fori_loop(0, 2, last, 0)
 
-    def collide(f, p):
+    def collide(f, p, pairs=range(1, 19, 2), rest=True):
         gas = flags[p] == 0
         vx, vy, wz = vel[1, p], vel[2, p], vel[3, p] + RELAX_TIME * GRAVITY
         base = 1.0 - 1.5 * (vx * vx + vy * vy + wz * wz)
         keep = jnp.where(gas, 0.0, 1.0 - 1.0 / RELAX_TIME)
         scale = jnp.where(gas, 0.0, vel[0, p] * (1.0 / RELAX_TIME))
-        new = {0: keep * f[0, p + 1] + (WEIGHTS[0] * scale) * base}
+        new = {0: keep * f[0, p + 1] + (WEIGHTS[0] * scale) * base} if rest else {}
         by_weight = {w: (w * scale, 3.0 * w * scale) for w in (WEIGHTS[1], WEIGHTS[7])}
-        for q in range(1, 19, 2):
+        for q in pairs:
             along = None
             for c, v in zip(VELOCITIES[q], (vx, vy, wz)):
                 if c:
@@ -487,14 +487,21 @@
     cross(0, f0, fz0, fz1.at[1], corner0)
 
     def first(p, acc):
-        new = collide(f0, p)
-        for q in range(19):
+        new = collide(f0, p, Z_PAIRS, False)
+        for q in new:
             f1[q, p + 1] = new[q]
         return pack_columns([new[q] for q in UP], [new[q] for q in DOWN], fz1[1, p + 1, 8:16], p, acc, lane)
+
+    def first_flat(p, c):
+        new = collide(f0, p, (1, 3, 7, 9))
+        for q in new:
+            f1[q, p + 1] = new[q]
+        return c
 
     store_z(1, lax.fori_loop(0, NP, first, acc0, unroll=8))
     corner1 = started(corner_sends(1))
     z1 = started(z_sends(1))
+    lax.fori_loop(0, NP, first_flat, 0, unroll=4)
     fill_x(1, f1, fz1)
     x1 = started(x_sends(1))
 

time: 28.3 us -> 28.1 us (level)
  no operation moved by 1% of the time
where the time goes in v6:
time: 28.1 us; the launch traced here: 27.9 us
  Pallas kernels  27.3 us (97%)
  between operations  0.64 us (2%)
    pallas_call x1, Pallas kernels, shards(): pl.pallas_call(fluid_kernel, out_shape=(jax.ShapeDtypeStruct((19, NP) + p...  25.3 us
    pallas_call x1, Pallas kernels, shards(): pl.pallas_call(finish_kernel, out_shape=(jax.ShapeDtypeStruct((19, NP) +...  2.01 us

profile of v6, /device:TPU:1, one launch (start us, length us, event | category | flops | bytes accessed | tf_op | source)
XLA Modules:
  0.0 27.9 jit_solution(17519597201584874175)
XLA Ops:
  0.6 25.3 %pour.1 = (f32[19,32,8,128]{3,2,1,0:T(8,128)S(1)}, f32[32,8,128]{2,1,0:T(8,128)S(1)}, f32[32,16,128]{2,1,0:T(8,128)S(1)}, f32[2,32,8,128]{3,2,1,0:T(8,128)S(1)}) custom-call(f32[19,32,8,128]{3,2,1,0:T(8,128)} %pops_in.1, f32[32,8,128]{2,1,0:T(8,128)} %fill_in.1, s32[32,8,128]{2,1,0:T(8,128)} %flags_in.1, f32[1,8,4096]{2,1,0:T(8,128)} %energy_in.3), custom_call_target="tpu_custom_call" | custom-call | tf_op jit(solution)/shard_map/pour/pallas_call | solution.py:706
  25.9 2.0 %finish.1 = (f32[19,32,8,128]{3,2,1,0:T(8,128)}, f32[32,8,128]{2,1,0:T(8,128)}, f32[1,8,4096]{2,1,0:T(8,128)}) custom-call(f32[19,32,8,128]{3,2,1,0:T(8,128)S(1)} %get-tuple-element.7.pops_mid, f32[32,8,128]{2,1,0:T(8,128)S(1)} %get-tuple-element.8.fill_mid, f32[32,16,128]{2,1,0:T(8,128)S(1)} %get-tuple-element.9.warm_mid, ...), custom_call_target="tpu_custom_call" | custom-call | tf_op jit(solution)/shard_map/finish/pallas_call | solution.py:755
